TPU v7x, 512 devices: a whole 4x4x16 slice. The times are simulated.
512 devices in a mesh: dp: 2 (over y_lo), ctx: 32 (over z, y_hi), tp: 8 (over x, core).
Axes of the slice: x: 4, y: 4 (y_hi: 2, y_lo: 2; y = y_hi * 2 + y_lo), z: 16, core: 2. Of those that a mesh axis runs over, the one named last changes fastest.
Arguments:
- queries: bfloat16 [8192, 3072], P(('dp', 'ctx'), 'tp'), parts along dimension 0, may hold values from -6 to 6
- query_tangent: bfloat16 [8192, 3072], P(('dp', 'ctx'), 'tp'), parts along dimension 0, may hold values from -6 to 6
- key_rows: bfloat16 [8192, 3072], P(('dp', 'ctx'), 'tp'), parts along dimension 0, may hold values from -6 to 6
- key_tangent: bfloat16 [8192, 3072], P(('dp', 'ctx'), 'tp'), parts along dimension 0, may hold values from -6 to 6
- value_rows: bfloat16 [8192, 3072], P(('dp', 'ctx'), 'tp'), parts along dimension 0, may hold values from -6 to 6
- value_tangent: bfloat16 [8192, 3072], P(('dp', 'ctx'), 'tp'), parts along dimension 0, may hold values from -6 to 6
- out_weight: bfloat16 [3072, 5120], P('tp'), may hold values from -0.15625 to 0.15625
- out_bias: float32 [5120], P('tp'), may hold values from -3 to 3
- gate_scale: float32 [10240], P(('dp', 'tp')), parts along dimension 0, may hold values from 0.1 to 1.9
- gate_tangent: float32 [10240], P(('dp', 'tp')), parts along dimension 0, may hold values from -6 to 6
Outputs:
- block_output: bfloat16 [8192, 5120], P(('dp', 'ctx'), 'tp'), parts along dimension 0
- output_tangent: bfloat16 [8192, 5120], P(('dp', 'ctx'), 'tp'), parts along dimension 0
There are 2 independent parts, one for each index of `dp`. A program takes and returns all parts, laid end to end along the dimension named above; an argument that names none is the same for every part. Nothing has to cross between parts.
All inputs are finite; a program needn't handle non-finite values.
Results may differ from a plain program's by a relative error of at most 0.02.
Values may be sent and summed in bfloat16 or wider, within the bound.
A program may use at most 64 MiB of HBM per device.

v0:
```python
import jax
import jax.numpy as jnp
from jax import lax
from jax.sharding import PartitionSpec as P

HD = 128


def passed_along(shard, axis, by):
    devices = lax.axis_size(axis)
    return lax.ppermute(shard, axis, [(i, (i + by) % devices) for i in range(devices)])


def absorb(state, block, local_query, local_tangent):
    top_score, total, slope, main_acc, value_acc, slope_acc = state
    factor = HD ** (-0.5)
    count = block.shape[1]
    heads = local_query.shape[1]
    keys = block[0].reshape(count, heads, HD)
    values = block[1].reshape(count, heads, HD)
    key_dot = block[2].reshape(count, heads, HD)
    value_dot = block[3].reshape(count, heads, HD)
    scores = (
        jnp.einsum("qhd,khd->qhk", local_query, keys, preferred_element_type=jnp.float32) * factor
    )
    tilt = (
        jnp.einsum("qhd,khd->qhk", local_tangent, keys, preferred_element_type=jnp.float32)
        + jnp.einsum("qhd,khd->qhk", local_query, key_dot, preferred_element_type=jnp.float32)
    ) * factor
    new_top = jnp.maximum(top_score, jnp.max(scores, axis=2))
    rescale = jnp.exp(top_score - new_top)
    weights = jnp.exp(scores - new_top[:, :, None])
    slanted = weights * tilt
    total = total * rescale + jnp.sum(weights, axis=2)
    slope = slope * rescale + jnp.sum(slanted, axis=2)
    rounded = weights.astype(jnp.bfloat16)
    tilted = slanted.astype(jnp.bfloat16)
    widened = rescale[:, :, None]
    main_acc = main_acc * widened + jnp.einsum(
        "qhk,khd->qhd", rounded, values, preferred_element_type=jnp.float32
    )
    value_acc = value_acc * widened + jnp.einsum(
        "qhk,khd->qhd", rounded, value_dot, preferred_element_type=jnp.float32
    )
    slope_acc = slope_acc * widened + jnp.einsum(
        "qhk,khd->qhd", tilted, values, preferred_element_type=jnp.float32
    )
    return (new_top, total, slope, main_acc, value_acc, slope_acc)


def per_device(
    queries,
    query_tangent,
    key_rows,
    key_tangent,
    value_rows,
    value_tangent,
    out_weight,
    out_bias,
    gate_scale,
    gate_tangent,
):
    rows = queries.shape[0]
    heads = queries.shape[1] // HD
    local_query = queries.reshape(rows, heads, HD)
    local_tangent = query_tangent.reshape(rows, heads, HD)
    block = jnp.stack([key_rows, value_rows, key_tangent, value_tangent])
    flat_zero = jnp.zeros((rows, heads), jnp.float32)
    wide_zero = jnp.zeros((rows, heads, HD), jnp.float32)
    start_state = (
        jnp.full((rows, heads), -jnp.inf, jnp.float32),
        flat_zero,
        flat_zero,
        wide_zero,
        wide_zero,
        wide_zero,
    )
    state = absorb(start_state, block, local_query, local_tangent)

    def single_turn(count, carry):
        moving, inner = carry
        moving = passed_along(moving, "ctx", 1)
        return (moving, absorb(inner, moving, local_query, local_tangent))

    moving, state = lax.fori_loop(0, lax.axis_size("ctx") - 1, single_turn, (block, state))
    top_score, total, slope, main_acc, value_acc, slope_acc = state
    attn = main_acc / total[:, :, None]
    attn_tangent = (slope_acc + value_acc) / total[:, :, None] - attn * (slope / total)[:, :, None]
    stacked = jnp.concatenate(
        [
            attn.reshape(rows, -1).astype(jnp.bfloat16),
            attn_tangent.reshape(rows, -1).astype(jnp.bfloat16),
        ],
        0,
    )
    summed = lax.psum_scatter(
        lax.dot_general(
            out_weight, stacked, (((0,), (1,)), ((), ())), preferred_element_type=jnp.float32
        ).astype(jnp.bfloat16),
        "tp",
        scatter_dimension=0,
        tiled=True,
    ).astype(jnp.float32)
    result = summed.T
    shifted = result[:rows] + out_bias[None, :]
    proj_tangent = result[rows:]
    block_output = (gate_scale[None, :] * shifted).astype(jnp.bfloat16)
    output_tangent = (gate_tangent[None, :] * shifted + gate_scale[None, :] * proj_tangent).astype(
        jnp.bfloat16
    )
    return (block_output, output_tangent)


def solution(mesh):
    in_specs = (
        P(("dp", "ctx"), "tp"),
        P(("dp", "ctx"), "tp"),
        P(("dp", "ctx"), "tp"),
        P(("dp", "ctx"), "tp"),
        P(("dp", "ctx"), "tp"),
        P(("dp", "ctx"), "tp"),
        P("tp", None),
        P("tp"),
        P(("dp", "tp")),
        P(("dp", "tp")),
    )
    out_specs = (P(("dp", "ctx"), "tp"), P(("dp", "ctx"), "tp"))
    return jax.shard_map(
        per_device, mesh=mesh, in_specs=in_specs, out_specs=out_specs, check_vma=False
    )
```

profile of v0, /device:TPU:1, one launch (start us, length us, event | category | flops | bytes accessed | tf_op | source)
XLA Modules:
  0.0 581.7 jit_solution(11902122406094174486)
XLA Ops:
  15.2 481.7 %while.22 = (s32[]{:T(128)}, bf16[4,128,384]{1,2,0:T(8,128)(2,1)S(1)}, f32[128,3]{0,1:T(4,128)S(1)}, f32[128,3]{0,1:T(4,128)S(1)}, f32[128,3]{0,1:T(4,128)S(1)},...) while((s32[]{:T(128)}, ...), condition=%wide.region_7.0_spmd, body=%wide.region_3.0_spmd.sunk | while | flops 76481664 | bytes 6821525 | solution.py:85
  15.2 5.7 collective-permute-start
  20.9 17.8 %collective-permute-done = bf16[4,128,384]{1,2,0:T(8,128)(2,1)S(1)} collective-permute-done((bf16[4,128,384]{1,2,0:T(8,128)(2,1)S(1)}, bf16[4,128,384]{1,2,0:T(8,128)(2,1)S(1)}, u32[]{:S(2)}, u32[]{:S(2)}) %collective-permute-start) | collective-permute-done | bytes 393248 | tf_op jit(solution)/shard_map/while/body/eval_jaxpr/ppermute | solution.py:11
  40.4 1.9 collective-permute-start
  42.3 13.0 %collective-permute-done = bf16[4,128,384]{1,2,0:T(8,128)(2,1)S(1)} collective-permute-done((bf16[4,128,384]{1,2,0:T(8,128)(2,1)S(1)}, bf16[4,128,384]{1,2,0:T(8,128)(2,1)S(1)}, u32[]{:S(2)}, u32[]{:S(2)}) %collective-permute-start) | collective-permute-done | bytes 393248 | tf_op jit(solution)/shard_map/while/body/eval_jaxpr/ppermute | solution.py:11
  58.9 12.0 %collective-permute-done = bf16[4,128,384]{1,2,0:T(8,128)(2,1)S(1)} collective-permute-done((bf16[4,128,384]{1,2,0:T(8,128)(2,1)S(1)}, bf16[4,128,384]{1,2,0:T(8,128)(2,1)S(1)}, u32[]{:S(2)}, u32[]{:S(2)}) %collective-permute-start) | collective-permute-done | bytes 393248 | tf_op jit(solution)/shard_map/while/body/eval_jaxpr/ppermute | solution.py:11
  74.6 11.1 %collective-permute-done = bf16[4,128,384]{1,2,0:T(8,128)(2,1)S(1)} collective-permute-done((bf16[4,128,384]{1,2,0:T(8,128)(2,1)S(1)}, bf16[4,128,384]{1,2,0:T(8,128)(2,1)S(1)}, u32[]{:S(2)}, u32[]{:S(2)}) %collective-permute-start) | collective-permute-done | bytes 393248 | tf_op jit(solution)/shard_map/while/body/eval_jaxpr/ppermute | solution.py:11
  89.4 10.2 %collective-permute-done = bf16[4,128,384]{1,2,0:T(8,128)(2,1)S(1)} collective-permute-done((bf16[4,128,384]{1,2,0:T(8,128)(2,1)S(1)}, bf16[4,128,384]{1,2,0:T(8,128)(2,1)S(1)}, u32[]{:S(2)}, u32[]{:S(2)}) %collective-permute-start) | collective-permute-done | bytes 393248 | tf_op jit(solution)/shard_map/while/body/eval_jaxpr/ppermute | solution.py:11
  101.3 1.9 collective-permute-start
  103.2 10.2 %collective-permute-done = bf16[4,128,384]{1,2,0:T(8,128)(2,1)S(1)} collective-permute-done((bf16[4,128,384]{1,2,0:T(8,128)(2,1)S(1)}, bf16[4,128,384]{1,2,0:T(8,128)(2,1)S(1)}, u32[]{:S(2)}, u32[]{:S(2)}) %collective-permute-start) | collective-permute-done | bytes 393248 | tf_op jit(solution)/shard_map/while/body/eval_jaxpr/ppermute | solution.py:11
  117.1 10.2 %collective-permute-done = bf16[4,128,384]{1,2,0:T(8,128)(2,1)S(1)} collective-permute-done((bf16[4,128,384]{1,2,0:T(8,128)(2,1)S(1)}, bf16[4,128,384]{1,2,0:T(8,128)(2,1)S(1)}, u32[]{:S(2)}, u32[]{:S(2)}) %collective-permute-start) | collective-permute-done | bytes 393248 | tf_op jit(solution)/shard_map/while/body/eval_jaxpr/ppermute | solution.py:11
  131.0 10.2 %collective-permute-done = bf16[4,128,384]{1,2,0:T(8,128)(2,1)S(1)} collective-permute-done((bf16[4,128,384]{1,2,0:T(8,128)(2,1)S(1)}, bf16[4,128,384]{1,2,0:T(8,128)(2,1)S(1)}, u32[]{:S(2)}, u32[]{:S(2)}) %collective-permute-start) | collective-permute-done | bytes 393248 | tf_op jit(solution)/shard_map/while/body/eval_jaxpr/ppermute | solution.py:11
  142.9 1.9 collective-permute-start
  144.8 10.2 %collective-permute-done = bf16[4,128,384]{1,2,0:T(8,128)(2,1)S(1)} collective-permute-done((bf16[4,128,384]{1,2,0:T(8,128)(2,1)S(1)}, bf16[4,128,384]{1,2,0:T(8,128)(2,1)S(1)}, u32[]{:S(2)}, u32[]{:S(2)}) %collective-permute-start) | collective-permute-done | bytes 393248 | tf_op jit(solution)/shard_map/while/body/eval_jaxpr/ppermute | solution.py:11
  158.7 10.2 %collective-permute-done = bf16[4,128,384]{1,2,0:T(8,128)(2,1)S(1)} collective-permute-done((bf16[4,128,384]{1,2,0:T(8,128)(2,1)S(1)}, bf16[4,128,384]{1,2,0:T(8,128)(2,1)S(1)}, u32[]{:S(2)}, u32[]{:S(2)}) %collective-permute-start) | collective-permute-done | bytes 393248 | tf_op jit(solution)/shard_map/while/body/eval_jaxpr/ppermute | solution.py:11
  170.6 1.9 collective-permute-start
  172.6 10.8 %collective-permute-done = bf16[4,128,384]{1,2,0:T(8,128)(2,1)S(1)} collective-permute-done((bf16[4,128,384]{1,2,0:T(8,128)(2,1)S(1)}, bf16[4,128,384]{1,2,0:T(8,128)(2,1)S(1)}, u32[]{:S(2)}, u32[]{:S(2)}) %collective-permute-start) | collective-permute-done | bytes 393248 | tf_op jit(solution)/shard_map/while/body/eval_jaxpr/ppermute | solution.py:11
  187.0 11.8 %collective-permute-done = bf16[4,128,384]{1,2,0:T(8,128)(2,1)S(1)} collective-permute-done((bf16[4,128,384]{1,2,0:T(8,128)(2,1)S(1)}, bf16[4,128,384]{1,2,0:T(8,128)(2,1)S(1)}, u32[]{:S(2)}, u32[]{:S(2)}) %collective-permute-start) | collective-permute-done | bytes 393248 | tf_op jit(solution)/shard_map/while/body/eval_jaxpr/ppermute | solution.py:11
  200.5 1.9 collective-permute-start
  202.5 12.9 %collective-permute-done = bf16[4,128,384]{1,2,0:T(8,128)(2,1)S(1)} collective-permute-done((bf16[4,128,384]{1,2,0:T(8,128)(2,1)S(1)}, bf16[4,128,384]{1,2,0:T(8,128)(2,1)S(1)}, u32[]{:S(2)}, u32[]{:S(2)}) %collective-permute-start) | collective-permute-done | bytes 393248 | tf_op jit(solution)/shard_map/while/body/eval_jaxpr/ppermute | solution.py:11
  219.1 14.0 %collective-permute-done = bf16[4,128,384]{1,2,0:T(8,128)(2,1)S(1)} collective-permute-done((bf16[4,128,384]{1,2,0:T(8,128)(2,1)S(1)}, bf16[4,128,384]{1,2,0:T(8,128)(2,1)S(1)}, u32[]{:S(2)}, u32[]{:S(2)}) %collective-permute-start) | collective-permute-done | bytes 393248 | tf_op jit(solution)/shard_map/while/body/eval_jaxpr/ppermute | solution.py:11
  236.7 13.9 %collective-permute-done = bf16[4,128,384]{1,2,0:T(8,128)(2,1)S(1)} collective-permute-done((bf16[4,128,384]{1,2,0:T(8,128)(2,1)S(1)}, bf16[4,128,384]{1,2,0:T(8,128)(2,1)S(1)}, u32[]{:S(2)}, u32[]{:S(2)}) %collective-permute-start) | collective-permute-done | bytes 393248 | tf_op jit(solution)/shard_map/while/body/eval_jaxpr/ppermute | solution.py:11
  254.3 13.0 %collective-permute-done = bf16[4,128,384]{1,2,0:T(8,128)(2,1)S(1)} collective-permute-done((bf16[4,128,384]{1,2,0:T(8,128)(2,1)S(1)}, bf16[4,128,384]{1,2,0:T(8,128)(2,1)S(1)}, u32[]{:S(2)}, u32[]{:S(2)}) %collective-permute-start) | collective-permute-done | bytes 393248 | tf_op jit(solution)/shard_map/while/body/eval_jaxpr/ppermute | solution.py:11
  269.0 1.9 collective-permute-start
  271.0 12.1 %collective-permute-done = bf16[4,128,384]{1,2,0:T(8,128)(2,1)S(1)} collective-permute-done((bf16[4,128,384]{1,2,0:T(8,128)(2,1)S(1)}, bf16[4,128,384]{1,2,0:T(8,128)(2,1)S(1)}, u32[]{:S(2)}, u32[]{:S(2)}) %collective-permute-start) | collective-permute-done | bytes 393248 | tf_op jit(solution)/shard_map/while/body/eval_jaxpr/ppermute | solution.py:11
  286.7 11.2 %collective-permute-done = bf16[4,128,384]{1,2,0:T(8,128)(2,1)S(1)} collective-permute-done((bf16[4,128,384]{1,2,0:T(8,128)(2,1)S(1)}, bf16[4,128,384]{1,2,0:T(8,128)(2,1)S(1)}, u32[]{:S(2)}, u32[]{:S(2)}) %collective-permute-start) | collective-permute-done | bytes 393248 | tf_op jit(solution)/shard_map/while/body/eval_jaxpr/ppermute | solution.py:11
  301.5 10.2 %collective-permute-done = bf16[4,128,384]{1,2,0:T(8,128)(2,1)S(1)} collective-permute-done((bf16[4,128,384]{1,2,0:T(8,128)(2,1)S(1)}, bf16[4,128,384]{1,2,0:T(8,128)(2,1)S(1)}, u32[]{:S(2)}, u32[]{:S(2)}) %collective-permute-start) | collective-permute-done | bytes 393248 | tf_op jit(solution)/shard_map/while/body/eval_jaxpr/ppermute | solution.py:11
  313.4 1.9 collective-permute-start
  315.4 10.2 %collective-permute-done = bf16[4,128,384]{1,2,0:T(8,128)(2,1)S(1)} collective-permute-done((bf16[4,128,384]{1,2,0:T(8,128)(2,1)S(1)}, bf16[4,128,384]{1,2,0:T(8,128)(2,1)S(1)}, u32[]{:S(2)}, u32[]{:S(2)}) %collective-permute-start) | collective-permute-done | bytes 393248 | tf_op jit(solution)/shard_map/while/body/eval_jaxpr/ppermute | solution.py:11
  329.2 10.2 %collective-permute-done = bf16[4,128,384]{1,2,0:T(8,128)(2,1)S(1)} collective-permute-done((bf16[4,128,384]{1,2,0:T(8,128)(2,1)S(1)}, bf16[4,128,384]{1,2,0:T(8,128)(2,1)S(1)}, u32[]{:S(2)}, u32[]{:S(2)}) %collective-permute-start) | collective-permute-done | bytes 393248 | tf_op jit(solution)/shard_map/while/body/eval_jaxpr/ppermute | solution.py:11
  343.1 10.2 %collective-permute-done = bf16[4,128,384]{1,2,0:T(8,128)(2,1)S(1)} collective-permute-done((bf16[4,128,384]{1,2,0:T(8,128)(2,1)S(1)}, bf16[4,128,384]{1,2,0:T(8,128)(2,1)S(1)}, u32[]{:S(2)}, u32[]{:S(2)}) %collective-permute-start) | collective-permute-done | bytes 393248 | tf_op jit(solution)/shard_map/while/body/eval_jaxpr/ppermute | solution.py:11
  355.0 1.9 collective-permute-start
  357.0 10.2 %collective-permute-done = bf16[4,128,384]{1,2,0:T(8,128)(2,1)S(1)} collective-permute-done((bf16[4,128,384]{1,2,0:T(8,128)(2,1)S(1)}, bf16[4,128,384]{1,2,0:T(8,128)(2,1)S(1)}, u32[]{:S(2)}, u32[]{:S(2)}) %collective-permute-start) | collective-permute-done | bytes 393248 | tf_op jit(solution)/shard_map/while/body/eval_jaxpr/ppermute | solution.py:11
  370.8 10.2 %collective-permute-done = bf16[4,128,384]{1,2,0:T(8,128)(2,1)S(1)} collective-permute-done((bf16[4,128,384]{1,2,0:T(8,128)(2,1)S(1)}, bf16[4,128,384]{1,2,0:T(8,128)(2,1)S(1)}, u32[]{:S(2)}, u32[]{:S(2)}) %collective-permute-start) | collective-permute-done | bytes 393248 | tf_op jit(solution)/shard_map/while/body/eval_jaxpr/ppermute | solution.py:11
  384.7 10.7 %collective-permute-done = bf16[4,128,384]{1,2,0:T(8,128)(2,1)S(1)} collective-permute-done((bf16[4,128,384]{1,2,0:T(8,128)(2,1)S(1)}, bf16[4,128,384]{1,2,0:T(8,128)(2,1)S(1)}, u32[]{:S(2)}, u32[]{:S(2)}) %collective-permute-start) | collective-permute-done | bytes 393248 | tf_op jit(solution)/shard_map/while/body/eval_jaxpr/ppermute | solution.py:11
  397.2 1.9 collective-permute-start
  399.1 11.8 %collective-permute-done = bf16[4,128,384]{1,2,0:T(8,128)(2,1)S(1)} collective-permute-done((bf16[4,128,384]{1,2,0:T(8,128)(2,1)S(1)}, bf16[4,128,384]{1,2,0:T(8,128)(2,1)S(1)}, u32[]{:S(2)}, u32[]{:S(2)}) %collective-permute-start) | collective-permute-done | bytes 393248 | tf_op jit(solution)/shard_map/while/body/eval_jaxpr/ppermute | solution.py:11
  412.6 1.9 collective-permute-start
  414.5 12.9 %collective-permute-done = bf16[4,128,384]{1,2,0:T(8,128)(2,1)S(1)} collective-permute-done((bf16[4,128,384]{1,2,0:T(8,128)(2,1)S(1)}, bf16[4,128,384]{1,2,0:T(8,128)(2,1)S(1)}, u32[]{:S(2)}, u32[]{:S(2)}) %collective-permute-start) | collective-permute-done | bytes 393248 | tf_op jit(solution)/shard_map/while/body/eval_jaxpr/ppermute | solution.py:11
  429.2 1.9 collective-permute-start
  431.1 14.0 %collective-permute-done = bf16[4,128,384]{1,2,0:T(8,128)(2,1)S(1)} collective-permute-done((bf16[4,128,384]{1,2,0:T(8,128)(2,1)S(1)}, bf16[4,128,384]{1,2,0:T(8,128)(2,1)S(1)}, u32[]{:S(2)}, u32[]{:S(2)}) %collective-permute-start) | collective-permute-done | bytes 393248 | tf_op jit(solution)/shard_map/while/body/eval_jaxpr/ppermute | solution.py:11
  446.8 1.9 collective-permute-start
  448.7 14.0 %collective-permute-done = bf16[4,128,384]{1,2,0:T(8,128)(2,1)S(1)} collective-permute-done((bf16[4,128,384]{1,2,0:T(8,128)(2,1)S(1)}, bf16[4,128,384]{1,2,0:T(8,128)(2,1)S(1)}, u32[]{:S(2)}, u32[]{:S(2)}) %collective-permute-start) | collective-permute-done | bytes 393248 | tf_op jit(solution)/shard_map/while/body/eval_jaxpr/ppermute | solution.py:11
  466.3 13.0 %collective-permute-done = bf16[4,128,384]{1,2,0:T(8,128)(2,1)S(1)} collective-permute-done((bf16[4,128,384]{1,2,0:T(8,128)(2,1)S(1)}, bf16[4,128,384]{1,2,0:T(8,128)(2,1)S(1)}, u32[]{:S(2)}, u32[]{:S(2)}) %collective-permute-start) | collective-permute-done | bytes 393248 | tf_op jit(solution)/shard_map/while/body/eval_jaxpr/ppermute | solution.py:11
  483.0 12.1 %collective-permute-done = bf16[4,128,384]{1,2,0:T(8,128)(2,1)S(1)} collective-permute-done((bf16[4,128,384]{1,2,0:T(8,128)(2,1)S(1)}, bf16[4,128,384]{1,2,0:T(8,128)(2,1)S(1)}, u32[]{:S(2)}, u32[]{:S(2)}) %collective-permute-start) | collective-permute-done | bytes 393248 | tf_op jit(solution)/shard_map/while/body/eval_jaxpr/ppermute | solution.py:11
  497.4 3.7 fusion.12
  501.1 2.6 copy.117
  503.7 69.1 %reduce-scatter.4.cloned.1.call-done = bf16[640,256]{1,0:T(8,128)(2,1)} async-done(((bf16[5120,256]{1,0:T(8,128)(2,1)}), bf16[640,256]{1,0:T(8,128)(2,1)}) %reduce-scatter.4.cloned.1.call-update) | async-done | bytes 327696
  (454 shorter events, 96.5 us)
Async XLA Ops:
  7.2 565.7 %reduce-scatter.4.cloned.1.call-start = ((), (), s32[]{:S(2)}) async-start(), calls=%async_computation.1 | async-start | bytes 2949120
  15.2 23.4 %collective-permute-start = (bf16[4,128,384]{1,2,0:T(8,128)(2,1)S(1)}, bf16[4,128,384]{1,2,0:T(8,128)(2,1)S(1)}, u32[]{:S(2)}, u32[]{:S(2)}) collective-permute-start(bf16[4,128,384]{1,2,0:T(8,128)(2,1)S(1)} %get-tuple-element.221), channel_id=1, source_target_pairs={{0,8},{8,16},{16,24},{24,32},{32,40},{40,48},{48,56},{56,64},{64,7... | collective-permute-start | bytes 1179656 | tf_op jit(solution)/shard_map/while/body/eval_jaxpr/ppermute | solution.py:11
  40.4 14.9 %collective-permute-start = (bf16[4,128,384]{1,2,0:T(8,128)(2,1)S(1)}, bf16[4,128,384]{1,2,0:T(8,128)(2,1)S(1)}, u32[]{:S(2)}, u32[]{:S(2)}) collective-permute-start(bf16[4,128,384]{1,2,0:T(8,128)(2,1)S(1)} %get-tuple-element.221), channel_id=1, source_target_pairs={{0,8},{8,16},{16,24},{24,32},{32,40},{40,48},{48,56},{56,64},{64,7... | collective-permute-start | bytes 1179656 | tf_op jit(solution)/shard_map/while/body/eval_jaxpr/ppermute | solution.py:11
  57.0 14.0 %collective-permute-start = (bf16[4,128,384]{1,2,0:T(8,128)(2,1)S(1)}, bf16[4,128,384]{1,2,0:T(8,128)(2,1)S(1)}, u32[]{:S(2)}, u32[]{:S(2)}) collective-permute-start(bf16[4,128,384]{1,2,0:T(8,128)(2,1)S(1)} %get-tuple-element.221), channel_id=1, source_target_pairs={{0,8},{8,16},{16,24},{24,32},{32,40},{40,48},{48,56},{56,64},{64,7... | collective-permute-start | bytes 1179656 | tf_op jit(solution)/shard_map/while/body/eval_jaxpr/ppermute | solution.py:11
  72.7 13.0 %collective-permute-start = (bf16[4,128,384]{1,2,0:T(8,128)(2,1)S(1)}, bf16[4,128,384]{1,2,0:T(8,128)(2,1)S(1)}, u32[]{:S(2)}, u32[]{:S(2)}) collective-permute-start(bf16[4,128,384]{1,2,0:T(8,128)(2,1)S(1)} %get-tuple-element.221), channel_id=1, source_target_pairs={{0,8},{8,16},{16,24},{24,32},{32,40},{40,48},{48,56},{56,64},{64,7... | collective-permute-start | bytes 1179656 | tf_op jit(solution)/shard_map/while/body/eval_jaxpr/ppermute | solution.py:11
  87.4 12.1 %collective-permute-start = (bf16[4,128,384]{1,2,0:T(8,128)(2,1)S(1)}, bf16[4,128,384]{1,2,0:T(8,128)(2,1)S(1)}, u32[]{:S(2)}, u32[]{:S(2)}) collective-permute-start(bf16[4,128,384]{1,2,0:T(8,128)(2,1)S(1)} %get-tuple-element.221), channel_id=1, source_target_pairs={{0,8},{8,16},{16,24},{24,32},{32,40},{40,48},{48,56},{56,64},{64,7... | collective-permute-start | bytes 1179656 | tf_op jit(solution)/shard_map/while/body/eval_jaxpr/ppermute | solution.py:11
  101.3 12.1 %collective-permute-start = (bf16[4,128,384]{1,2,0:T(8,128)(2,1)S(1)}, bf16[4,128,384]{1,2,0:T(8,128)(2,1)S(1)}, u32[]{:S(2)}, u32[]{:S(2)}) collective-permute-start(bf16[4,128,384]{1,2,0:T(8,128)(2,1)S(1)} %get-tuple-element.221), channel_id=1, source_target_pairs={{0,8},{8,16},{16,24},{24,32},{32,40},{40,48},{48,56},{56,64},{64,7... | collective-permute-start | bytes 1179656 | tf_op jit(solution)/shard_map/while/body/eval_jaxpr/ppermute | solution.py:11
  115.2 12.1 %collective-permute-start = (bf16[4,128,384]{1,2,0:T(8,128)(2,1)S(1)}, bf16[4,128,384]{1,2,0:T(8,128)(2,1)S(1)}, u32[]{:S(2)}, u32[]{:S(2)}) collective-permute-start(bf16[4,128,384]{1,2,0:T(8,128)(2,1)S(1)} %get-tuple-element.221), channel_id=1, source_target_pairs={{0,8},{8,16},{16,24},{24,32},{32,40},{40,48},{48,56},{56,64},{64,7... | collective-permute-start | bytes 1179656 | tf_op jit(solution)/shard_map/while/body/eval_jaxpr/ppermute | solution.py:11
  129.0 12.1 %collective-permute-start = (bf16[4,128,384]{1,2,0:T(8,128)(2,1)S(1)}, bf16[4,128,384]{1,2,0:T(8,128)(2,1)S(1)}, u32[]{:S(2)}, u32[]{:S(2)}) collective-permute-start(bf16[4,128,384]{1,2,0:T(8,128)(2,1)S(1)} %get-tuple-element.221), channel_id=1, source_target_pairs={{0,8},{8,16},{16,24},{24,32},{32,40},{40,48},{48,56},{56,64},{64,7... | collective-permute-start | bytes 1179656 | tf_op jit(solution)/shard_map/while/body/eval_jaxpr/ppermute | solution.py:11
  142.9 12.1 %collective-permute-start = (bf16[4,128,384]{1,2,0:T(8,128)(2,1)S(1)}, bf16[4,128,384]{1,2,0:T(8,128)(2,1)S(1)}, u32[]{:S(2)}, u32[]{:S(2)}) collective-permute-start(bf16[4,128,384]{1,2,0:T(8,128)(2,1)S(1)} %get-tuple-element.221), channel_id=1, source_target_pairs={{0,8},{8,16},{16,24},{24,32},{32,40},{40,48},{48,56},{56,64},{64,7... | collective-permute-start | bytes 1179656 | tf_op jit(solution)/shard_map/while/body/eval_jaxpr/ppermute | solution.py:11
  156.8 12.1 %collective-permute-start = (bf16[4,128,384]{1,2,0:T(8,128)(2,1)S(1)}, bf16[4,128,384]{1,2,0:T(8,128)(2,1)S(1)}, u32[]{:S(2)}, u32[]{:S(2)}) collective-permute-start(bf16[4,128,384]{1,2,0:T(8,128)(2,1)S(1)} %get-tuple-element.221), channel_id=1, source_target_pairs={{0,8},{8,16},{16,24},{24,32},{32,40},{40,48},{48,56},{56,64},{64,7... | collective-permute-start | bytes 1179656 | tf_op jit(solution)/shard_map/while/body/eval_jaxpr/ppermute | solution.py:11
  170.6 12.7 %collective-permute-start = (bf16[4,128,384]{1,2,0:T(8,128)(2,1)S(1)}, bf16[4,128,384]{1,2,0:T(8,128)(2,1)S(1)}, u32[]{:S(2)}, u32[]{:S(2)}) collective-permute-start(bf16[4,128,384]{1,2,0:T(8,128)(2,1)S(1)} %get-tuple-element.221), channel_id=1, source_target_pairs={{0,8},{8,16},{16,24},{24,32},{32,40},{40,48},{48,56},{56,64},{64,7... | collective-permute-start | bytes 1179656 | tf_op jit(solution)/shard_map/while/body/eval_jaxpr/ppermute | solution.py:11
  185.0 13.8 %collective-permute-start = (bf16[4,128,384]{1,2,0:T(8,128)(2,1)S(1)}, bf16[4,128,384]{1,2,0:T(8,128)(2,1)S(1)}, u32[]{:S(2)}, u32[]{:S(2)}) collective-permute-start(bf16[4,128,384]{1,2,0:T(8,128)(2,1)S(1)} %get-tuple-element.221), channel_id=1, source_target_pairs={{0,8},{8,16},{16,24},{24,32},{32,40},{40,48},{48,56},{56,64},{64,7... | collective-permute-start | bytes 1179656 | tf_op jit(solution)/shard_map/while/body/eval_jaxpr/ppermute | solution.py:11
  200.5 14.9 %collective-permute-start = (bf16[4,128,384]{1,2,0:T(8,128)(2,1)S(1)}, bf16[4,128,384]{1,2,0:T(8,128)(2,1)S(1)}, u32[]{:S(2)}, u32[]{:S(2)}) collective-permute-start(bf16[4,128,384]{1,2,0:T(8,128)(2,1)S(1)} %get-tuple-element.221), channel_id=1, source_target_pairs={{0,8},{8,16},{16,24},{24,32},{32,40},{40,48},{48,56},{56,64},{64,7... | collective-permute-start | bytes 1179656 | tf_op jit(solution)/shard_map/while/body/eval_jaxpr/ppermute | solution.py:11
  217.1 15.9 %collective-permute-start = (bf16[4,128,384]{1,2,0:T(8,128)(2,1)S(1)}, bf16[4,128,384]{1,2,0:T(8,128)(2,1)S(1)}, u32[]{:S(2)}, u32[]{:S(2)}) collective-permute-start(bf16[4,128,384]{1,2,0:T(8,128)(2,1)S(1)} %get-tuple-element.221), channel_id=1, source_target_pairs={{0,8},{8,16},{16,24},{24,32},{32,40},{40,48},{48,56},{56,64},{64,7... | collective-permute-start | bytes 1179656 | tf_op jit(solution)/shard_map/while/body/eval_jaxpr/ppermute | solution.py:11
  234.8 15.9 %collective-permute-start = (bf16[4,128,384]{1,2,0:T(8,128)(2,1)S(1)}, bf16[4,128,384]{1,2,0:T(8,128)(2,1)S(1)}, u32[]{:S(2)}, u32[]{:S(2)}) collective-permute-start(bf16[4,128,384]{1,2,0:T(8,128)(2,1)S(1)} %get-tuple-element.221), channel_id=1, source_target_pairs={{0,8},{8,16},{16,24},{24,32},{32,40},{40,48},{48,56},{56,64},{64,7... | collective-permute-start | bytes 1179656 | tf_op jit(solution)/shard_map/while/body/eval_jaxpr/ppermute | solution.py:11
  252.4 14.9 %collective-permute-start = (bf16[4,128,384]{1,2,0:T(8,128)(2,1)S(1)}, bf16[4,128,384]{1,2,0:T(8,128)(2,1)S(1)}, u32[]{:S(2)}, u32[]{:S(2)}) collective-permute-start(bf16[4,128,384]{1,2,0:T(8,128)(2,1)S(1)} %get-tuple-element.221), channel_id=1, source_target_pairs={{0,8},{8,16},{16,24},{24,32},{32,40},{40,48},{48,56},{56,64},{64,7... | collective-permute-start | bytes 1179656 | tf_op jit(solution)/shard_map/while/body/eval_jaxpr/ppermute | solution.py:11
  269.0 14.0 %collective-permute-start = (bf16[4,128,384]{1,2,0:T(8,128)(2,1)S(1)}, bf16[4,128,384]{1,2,0:T(8,128)(2,1)S(1)}, u32[]{:S(2)}, u32[]{:S(2)}) collective-permute-start(bf16[4,128,384]{1,2,0:T(8,128)(2,1)S(1)} %get-tuple-element.221), channel_id=1, source_target_pairs={{0,8},{8,16},{16,24},{24,32},{32,40},{40,48},{48,56},{56,64},{64,7... | collective-permute-start | bytes 1179656 | tf_op jit(solution)/shard_map/while/body/eval_jaxpr/ppermute | solution.py:11
  284.8 13.1 %collective-permute-start = (bf16[4,128,384]{1,2,0:T(8,128)(2,1)S(1)}, bf16[4,128,384]{1,2,0:T(8,128)(2,1)S(1)}, u32[]{:S(2)}, u32[]{:S(2)}) collective-permute-start(bf16[4,128,384]{1,2,0:T(8,128)(2,1)S(1)} %get-tuple-element.221), channel_id=1, source_target_pairs={{0,8},{8,16},{16,24},{24,32},{32,40},{40,48},{48,56},{56,64},{64,7... | collective-permute-start | bytes 1179656 | tf_op jit(solution)/shard_map/while/body/eval_jaxpr/ppermute | solution.py:11
  299.6 12.1 %collective-permute-start = (bf16[4,128,384]{1,2,0:T(8,128)(2,1)S(1)}, bf16[4,128,384]{1,2,0:T(8,128)(2,1)S(1)}, u32[]{:S(2)}, u32[]{:S(2)}) collective-permute-start(bf16[4,128,384]{1,2,0:T(8,128)(2,1)S(1)} %get-tuple-element.221), channel_id=1, source_target_pairs={{0,8},{8,16},{16,24},{24,32},{32,40},{40,48},{48,56},{56,64},{64,7... | collective-permute-start | bytes 1179656 | tf_op jit(solution)/shard_map/while/body/eval_jaxpr/ppermute | solution.py:11
  313.4 12.1 %collective-permute-start = (bf16[4,128,384]{1,2,0:T(8,128)(2,1)S(1)}, bf16[4,128,384]{1,2,0:T(8,128)(2,1)S(1)}, u32[]{:S(2)}, u32[]{:S(2)}) collective-permute-start(bf16[4,128,384]{1,2,0:T(8,128)(2,1)S(1)} %get-tuple-element.221), channel_id=1, source_target_pairs={{0,8},{8,16},{16,24},{24,32},{32,40},{40,48},{48,56},{56,64},{64,7... | collective-permute-start | bytes 1179656 | tf_op jit(solution)/shard_map/while/body/eval_jaxpr/ppermute | solution.py:11
  327.3 12.1 %collective-permute-start = (bf16[4,128,384]{1,2,0:T(8,128)(2,1)S(1)}, bf16[4,128,384]{1,2,0:T(8,128)(2,1)S(1)}, u32[]{:S(2)}, u32[]{:S(2)}) collective-permute-start(bf16[4,128,384]{1,2,0:T(8,128)(2,1)S(1)} %get-tuple-element.221), channel_id=1, source_target_pairs={{0,8},{8,16},{16,24},{24,32},{32,40},{40,48},{48,56},{56,64},{64,7... | collective-permute-start | bytes 1179656 | tf_op jit(solution)/shard_map/while/body/eval_jaxpr/ppermute | solution.py:11
  341.2 12.1 %collective-permute-start = (bf16[4,128,384]{1,2,0:T(8,128)(2,1)S(1)}, bf16[4,128,384]{1,2,0:T(8,128)(2,1)S(1)}, u32[]{:S(2)}, u32[]{:S(2)}) collective-permute-start(bf16[4,128,384]{1,2,0:T(8,128)(2,1)S(1)} %get-tuple-element.221), channel_id=1, source_target_pairs={{0,8},{8,16},{16,24},{24,32},{32,40},{40,48},{48,56},{56,64},{64,7... | collective-permute-start | bytes 1179656 | tf_op jit(solution)/shard_map/while/body/eval_jaxpr/ppermute | solution.py:11
  355.0 12.1 %collective-permute-start = (bf16[4,128,384]{1,2,0:T(8,128)(2,1)S(1)}, bf16[4,128,384]{1,2,0:T(8,128)(2,1)S(1)}, u32[]{:S(2)}, u32[]{:S(2)}) collective-permute-start(bf16[4,128,384]{1,2,0:T(8,128)(2,1)S(1)} %get-tuple-element.221), channel_id=1, source_target_pairs={{0,8},{8,16},{16,24},{24,32},{32,40},{40,48},{48,56},{56,64},{64,7... | collective-permute-start | bytes 1179656 | tf_op jit(solution)/shard_map/while/body/eval_jaxpr/ppermute | solution.py:11
  368.9 12.1 %collective-permute-start = (bf16[4,128,384]{1,2,0:T(8,128)(2,1)S(1)}, bf16[4,128,384]{1,2,0:T(8,128)(2,1)S(1)}, u32[]{:S(2)}, u32[]{:S(2)}) collective-permute-start(bf16[4,128,384]{1,2,0:T(8,128)(2,1)S(1)} %get-tuple-element.221), channel_id=1, source_target_pairs={{0,8},{8,16},{16,24},{24,32},{32,40},{40,48},{48,56},{56,64},{64,7... | collective-permute-start | bytes 1179656 | tf_op jit(solution)/shard_map/while/body/eval_jaxpr/ppermute | solution.py:11
  382.8 12.7 %collective-permute-start = (bf16[4,128,384]{1,2,0:T(8,128)(2,1)S(1)}, bf16[4,128,384]{1,2,0:T(8,128)(2,1)S(1)}, u32[]{:S(2)}, u32[]{:S(2)}) collective-permute-start(bf16[4,128,384]{1,2,0:T(8,128)(2,1)S(1)} %get-tuple-element.221), channel_id=1, source_target_pairs={{0,8},{8,16},{16,24},{24,32},{32,40},{40,48},{48,56},{56,64},{64,7... | collective-permute-start | bytes 1179656 | tf_op jit(solution)/shard_map/while/body/eval_jaxpr/ppermute | solution.py:11
  397.2 13.7 %collective-permute-start = (bf16[4,128,384]{1,2,0:T(8,128)(2,1)S(1)}, bf16[4,128,384]{1,2,0:T(8,128)(2,1)S(1)}, u32[]{:S(2)}, u32[]{:S(2)}) collective-permute-start(bf16[4,128,384]{1,2,0:T(8,128)(2,1)S(1)} %get-tuple-element.221), channel_id=1, source_target_pairs={{0,8},{8,16},{16,24},{24,32},{32,40},{40,48},{48,56},{56,64},{64,7... | collective-permute-start | bytes 1179656 | tf_op jit(solution)/shard_map/while/body/eval_jaxpr/ppermute | solution.py:11
  412.6 14.8 %collective-permute-start = (bf16[4,128,384]{1,2,0:T(8,128)(2,1)S(1)}, bf16[4,128,384]{1,2,0:T(8,128)(2,1)S(1)}, u32[]{:S(2)}, u32[]{:S(2)}) collective-permute-start(bf16[4,128,384]{1,2,0:T(8,128)(2,1)S(1)} %get-tuple-element.221), channel_id=1, source_target_pairs={{0,8},{8,16},{16,24},{24,32},{32,40},{40,48},{48,56},{56,64},{64,7... | collective-permute-start | bytes 1179656 | tf_op jit(solution)/shard_map/while/body/eval_jaxpr/ppermute | solution.py:11
  429.2 15.9 %collective-permute-start = (bf16[4,128,384]{1,2,0:T(8,128)(2,1)S(1)}, bf16[4,128,384]{1,2,0:T(8,128)(2,1)S(1)}, u32[]{:S(2)}, u32[]{:S(2)}) collective-permute-start(bf16[4,128,384]{1,2,0:T(8,128)(2,1)S(1)} %get-tuple-element.221), channel_id=1, source_target_pairs={{0,8},{8,16},{16,24},{24,32},{32,40},{40,48},{48,56},{56,64},{64,7... | collective-permute-start | bytes 1179656 | tf_op jit(solution)/shard_map/while/body/eval_jaxpr/ppermute | solution.py:11
  446.8 15.9 %collective-permute-start = (bf16[4,128,384]{1,2,0:T(8,128)(2,1)S(1)}, bf16[4,128,384]{1,2,0:T(8,128)(2,1)S(1)}, u32[]{:S(2)}, u32[]{:S(2)}) collective-permute-start(bf16[4,128,384]{1,2,0:T(8,128)(2,1)S(1)} %get-tuple-element.221), channel_id=1, source_target_pairs={{0,8},{8,16},{16,24},{24,32},{32,40},{40,48},{48,56},{56,64},{64,7... | collective-permute-start | bytes 1179656 | tf_op jit(solution)/shard_map/while/body/eval_jaxpr/ppermute | solution.py:11
  464.4 15.0 %collective-permute-start = (bf16[4,128,384]{1,2,0:T(8,128)(2,1)S(1)}, bf16[4,128,384]{1,2,0:T(8,128)(2,1)S(1)}, u32[]{:S(2)}, u32[]{:S(2)}) collective-permute-start(bf16[4,128,384]{1,2,0:T(8,128)(2,1)S(1)} %get-tuple-element.221), channel_id=1, source_target_pairs={{0,8},{8,16},{16,24},{24,32},{32,40},{40,48},{48,56},{56,64},{64,7... | collective-permute-start | bytes 1179656 | tf_op jit(solution)/shard_map/while/body/eval_jaxpr/ppermute | solution.py:11
  481.1 14.0 %collective-permute-start = (bf16[4,128,384]{1,2,0:T(8,128)(2,1)S(1)}, bf16[4,128,384]{1,2,0:T(8,128)(2,1)S(1)}, u32[]{:S(2)}, u32[]{:S(2)}) collective-permute-start(bf16[4,128,384]{1,2,0:T(8,128)(2,1)S(1)} %get-tuple-element.221), channel_id=1, source_target_pairs={{0,8},{8,16},{16,24},{24,32},{32,40},{40,48},{48,56},{56,64},{64,7... | collective-permute-start | bytes 1179656 | tf_op jit(solution)/shard_map/while/body/eval_jaxpr/ppermute | solution.py:11
  501.0 73.0 %copy-start = (f32[640]{0:T(1024)S(1)}, f32[640]{0:T(1024)}, u32[]{:S(2)}) copy-start(f32[640]{0:T(1024)} %param.21) | copy-start | bytes 7684
  501.0 73.0 %copy-start.1 = (f32[640]{0:T(1024)S(1)}, f32[640]{0:T(1024)}, u32[]{:S(2)}) copy-start(f32[640]{0:T(1024)} %param.19) | copy-start | bytes 7684
  501.1 73.0 %copy-start.2 = (f32[640]{0:T(1024)S(1)}, f32[640]{0:T(1024)}, u32[]{:S(2)}) copy-start(f32[640]{0:T(1024)} %param.20) | copy-start | bytes 7684
Sparse Core Ops, SparseCore 0:
  503.8 68.9 reduce-scatter.3
where the time goes:
time: 584 us; the launch traced here: 582 us
  waiting for transfers between devices  434 us (74%)
  starting transfers between devices  63.3 us (11%)
  matrix products  52.2 us (9%)
  between operations  14.2 us (2%)
  local copies, waits for them, and re-layouts  12.2 us (2%)
    ppermute x31, waiting for transfers between devices, passed_along(): lax.ppermute(shard, axis, [(i, (i + by) % devices) for i in range(devices)])  365 us
    unnamed x2, waiting for transfers between devices  69.2 us
    ppermute x31, starting transfers between devices, passed_along(): lax.ppermute(shard, axis, [(i, (i + by) % devices) for i in range(devices)])  63.3 us
  transfers between devices with their start and end apart: 32, of which 32 were waited for; matrix products, arithmetic and copies ran while one was open for 0% of the time, Pallas kernels for 0%

commit v1 on v0

v1 whole, which is shorter than its diff:
```python
import math

import jax
import jax.numpy as jnp
from jax import lax
from jax.experimental import pallas as pl
from jax.experimental.pallas import tpu as pltpu
from jax.sharding import PartitionSpec as P

HD = 128
HEADS = 3
ROWS = 128
HALF = ROWS // 2
RING = 16
STEPS = RING // 2
TP = 8
COLS = 640
FACTOR = HD ** (-0.5)
EXP_SCALE = FACTOR * math.log2(math.e)
MESH = pl.DeviceIdType.MESH
F32 = jnp.float32
BF16 = jnp.bfloat16


def dot_nt(a, b):
    return lax.dot_general(a, b, (((1,), (1,)), ((), ())), preferred_element_type=F32)


def kernel(
    q_ref, qt_ref, k_ref, kt_ref, v_ref, vt_ref, w_ref, bias_ref, scale_ref, slope_ref,
    out_ref, outt_ref,
    kv, qbuf, wbuf, att, proj, top, tot, slp, acc, acct,
    own_part, own_stat, part_out, part_in, stat_out, stat_in,
    ring_send, ring_recv, q_send, q_recv, w_send, w_recv, w_own,
    part_ssem, part_rsem, stat_ssem, stat_rsem, att_send, att_recv,
):
    ctx = lax.axis_index("ctx")
    tp = lax.axis_index("tp")
    z, y = ctx // 2, ctx % 2
    right = lax.rem(z + 1, RING) * 2 + y
    left = lax.rem(z + RING - 1, RING) * 2 + y
    partner = z * 2 + (1 - y)
    peers = [lax.rem(tp + i, TP) for i in range(1, TP)]

    barrier = pltpu.get_barrier_semaphore()
    for where in [{"ctx": right}, {"ctx": left}, {"ctx": partner}] + [{"tp": p} for p in peers]:
        pl.semaphore_signal(barrier, inc=1, device_id=where, device_id_type=MESH)

    for h in range(HEADS):
        cols = slice(h * HD, (h + 1) * HD)
        for i, ref in enumerate((k_ref, kt_ref, v_ref, vt_ref)):
            kv[h, 0, 0:ROWS, i * HD:(i + 1) * HD] = ref[:, cols]
        qbuf[h, 0:ROWS, 0:HD] = qt_ref[:, cols]
        qbuf[h, 0:ROWS, HD:2 * HD] = q_ref[:, cols]

    def ring(h, s, d, c):
        lo = c * HALF
        if isinstance(s, int) and s == STEPS:
            src = kv.at[h, STEPS - 1, pl.ds(d * ROWS + lo, HALF)]
            dst = kv.at[h, 0, pl.ds(ROWS + lo, HALF)]
        else:
            first = isinstance(s, int) and s == 1
            src = kv.at[h, s - 1, pl.ds((0 if first else d * ROWS) + lo, HALF)]
            dst = kv.at[h, s, pl.ds(d * ROWS + lo, HALF)]
        return pltpu.make_async_remote_copy(
            src_ref=src, dst_ref=dst,
            send_sem=ring_send.at[h, s - 1, d, c], recv_sem=ring_recv.at[h, s - 1, d, c],
            device_id={"ctx": right if d == 0 else left}, device_id_type=MESH)

    def start_ring(h):
        for c in range(2):
            for d in range(2):
                ring(h, 1, d, c).start()

    def q_copy(h):
        return pltpu.make_async_remote_copy(
            src_ref=qbuf.at[h, pl.ds(0, ROWS)], dst_ref=qbuf.at[h, pl.ds(ROWS, ROWS)],
            send_sem=q_send.at[h], recv_sem=q_recv.at[h],
            device_id={"ctx": partner}, device_id_type=MESH)

    def w_copy(i):
        peer = lax.rem(tp + i + 1, TP)
        return pltpu.make_async_remote_copy(
            src_ref=w_ref.at[:, :, pl.ds(pl.multiple_of(peer * COLS, COLS), COLS)],
            dst_ref=wbuf.at[:, pl.ds(pl.multiple_of(tp * HD, HD), HD), :],
            send_sem=w_send.at[i], recv_sem=w_recv.at[i],
            device_id={"tp": peer}, device_id_type=MESH)

    def att_copy(h, i):
        peer = lax.rem(tp + i + 1, TP)
        mine = att.at[h, :, pl.ds(pl.multiple_of(tp * HD, HD), HD)]
        return pltpu.make_async_remote_copy(
            src_ref=mine, dst_ref=mine,
            send_sem=att_send.at[h, i], recv_sem=att_recv.at[h, i],
            device_id={"tp": peer}, device_id_type=MESH)

    def part_copy(h):
        return pltpu.make_async_remote_copy(
            src_ref=part_out.at[h], dst_ref=part_in.at[h],
            send_sem=part_ssem.at[h], recv_sem=part_rsem.at[h],
            device_id={"ctx": partner}, device_id_type=MESH)

    def stat_copy(h):
        return pltpu.make_async_remote_copy(
            src_ref=stat_out.at[h], dst_ref=stat_in.at[h],
            send_sem=stat_ssem.at[h], recv_sem=stat_rsem.at[h],
            device_id={"ctx": partner}, device_id_type=MESH)

    own_w = pltpu.make_async_copy(
        w_ref.at[:, :, pl.ds(pl.multiple_of(tp * COLS, COLS), COLS)],
        wbuf.at[:, pl.ds(pl.multiple_of(tp * HD, HD), HD), :], w_own)

    pl.semaphore_wait(barrier, 3 + TP - 1)
    start_ring(0)
    for h in range(HEADS):
        q_copy(h).start()
    for i in range(TP - 1):
        w_copy(i).start()
    own_w.start()

    def attend(h, block, first=False):
        pair = qbuf[h]
        keys = block[:, 0:2 * HD]
        scores = dot_nt(pair[:, HD:], keys[:, :HD])
        tilt = dot_nt(pair, keys)
        count = scores.shape[1]
        peak = jnp.max(scores, axis=1, keepdims=True)
        if first:
            new = jnp.broadcast_to(peak, (2 * ROWS, HD))
        else:
            old = top[...]
            new = jnp.maximum(old, peak)
            shrink = jnp.exp2((old - new) * EXP_SCALE)
        top[...] = new
        wide = jnp.concatenate([new] * (count // HD), axis=1) if count > HD else new
        weights = jnp.exp2((scores - wide) * EXP_SCALE)
        slanted = weights * tilt
        folded, tilted = weights[:, :HD], slanted[:, :HD]
        for i in range(1, count // HD):
            folded = folded + weights[:, i * HD:(i + 1) * HD]
            tilted = tilted + slanted[:, i * HD:(i + 1) * HD]
        values = block[:, 2 * HD:]
        both = jnp.dot(weights.astype(BF16), values, preferred_element_type=F32)
        bent = jnp.dot(slanted.astype(BF16), values[:, :HD], preferred_element_type=F32)
        if first:
            tot[...] = folded
            slp[...] = tilted
            acc[...] = both
            acct[...] = bent
        else:
            tot[...] = tot[...] * shrink + folded
            slp[...] = slp[...] * shrink + tilted
            acc[...] = acc[...] * jnp.concatenate([shrink, shrink], axis=1) + both
            acct[...] = acct[...] * shrink + bent

    def part_of(h):
        total = jnp.sum(tot[...], axis=1, keepdims=True)
        incline = jnp.sum(slp[...], axis=1, keepdims=True) * FACTOR
        inverse = 1.0 / total
        incline = incline * inverse
        main = acc[:, :HD] * inverse
        tangent = (acct[...] * FACTOR + acc[:, HD:]) * inverse - main * incline
        own_part[h, :, :HD] = main[:ROWS]
        own_part[h, :, HD:] = tangent[:ROWS]
        part_out[h, :, :HD] = main[ROWS:].astype(BF16)
        part_out[h, :, HD:] = tangent[ROWS:].astype(BF16)
        part_copy(h).start()
        lane = lax.broadcasted_iota(jnp.int32, (ROWS, HD), 1)
        stat = jnp.where(lane == 0, top[ROWS:, :], jnp.where(lane == 1, total[ROWS:], incline[ROWS:]))
        stat_out[h] = stat.T[0:8]
        stat_copy(h).start()
        own_stat[h, 0] = top[0:ROWS, :]
        own_stat[h, 1] = jnp.broadcast_to(total[:ROWS], (ROWS, HD))
        own_stat[h, 2] = jnp.broadcast_to(incline[:ROWS], (ROWS, HD))

    def join(h):
        stat_copy(h).wait_recv()
        part_copy(h).wait_recv()
        theirs = jnp.concatenate([stat_in[h]] * (HD // 8), axis=0).T
        top1, total1, incline1 = theirs[:, 0:1], theirs[:, 1:2], theirs[:, 2:3]
        top0, total0, incline0 = own_stat[h, 0], own_stat[h, 1], own_stat[h, 2]
        high = jnp.maximum(top0, top1)
        share0 = total0 * jnp.exp2((top0 - high) * EXP_SCALE)
        share1 = total1 * jnp.exp2((top1 - high) * EXP_SCALE)
        inverse = 1.0 / (share0 + share1)
        share0 = share0 * inverse
        share1 = share1 * inverse
        incline = share0 * incline0 + share1 * incline1
        main0, tan0 = own_part[h, :, :HD], own_part[h, :, HD:]
        main1, tan1 = part_in[h, :, :HD].astype(F32), part_in[h, :, HD:].astype(F32)
        main = share0 * main0 + share1 * main1
        tangent = (share0 * (tan0 + main0 * (incline0 - incline))
                   + share1 * (tan1 + main1 * (incline1 - incline)))
        cols = pl.ds(pl.multiple_of(tp * HD, HD), HD)
        att[h, 0:ROWS, cols] = main.astype(BF16)
        att[h, ROWS:2 * ROWS, cols] = tangent.astype(BF16)
        for i in range(TP - 1):
            att_copy(h, i).start()

    def project(h):
        for i in range(TP - 1):
            att_copy(h, i).wait_recv()
        if h == 0:
            own_w.wait()
            for i in range(TP - 1):
                w_copy(i).wait_recv()
        term = jnp.dot(att[h], wbuf[h], preferred_element_type=F32)
        if h == 0:
            proj[...] = term
        else:
            proj[...] += term

    def pass_on(h, s, sends=((0, 0), (0, 1), (1, 0), (1, 1))):
        for c in range(2):
            for d in range(2):
                ring(h, s, d, c).wait_recv()
                if (c, d) in sends:
                    ring(h, s + 1, d, c).start()

    for h in range(HEADS):
        if h == 0:
            pass_on(0, 1)
            pass_on(0, 2)
            for i in range(HEADS):
                q_copy(i).wait_recv()
            attend(0, kv.at[0, 0, pl.ds(0, ROWS)], first=True)
            attend(0, kv.at[0, 1])
            attend(0, kv.at[0, 2])
            begin = 3
        else:
            attend(h, kv.at[h, 0, pl.ds(0, ROWS)], first=True)
            begin = 1

        def turn(s, carry, h=h):
            pass_on(h, s)
            attend(h, kv.at[h, s])
            return carry

        if begin == 1:
            pass_on(h, 1)
            attend(h, kv.at[h, 1])
            begin = 2
        lax.fori_loop(begin, 4, turn, 0)
        if h > 0:
            join(h - 1)
        lax.fori_loop(4, STEPS - 1, turn, 0)
        pass_on(h, STEPS - 1, sends=((0, 0), (1, 1)))
        if h + 1 < HEADS:
            start_ring(h + 1)
        attend(h, kv.at[h, STEPS - 1])
        ring(h, STEPS, 0, 0).wait_recv()
        ring(h, STEPS, 1, 1).wait_recv()
        attend(h, kv.at[h, 0, pl.ds(ROWS, ROWS)])
        part_of(h)

    project(0)
    project(1)
    join(HEADS - 1)
    project(HEADS - 1)

    shifted = proj[0:ROWS, :] + bias_ref[...]
    out_ref[...] = (scale_ref[...] * shifted).astype(BF16)
    outt_ref[...] = (slope_ref[...] * shifted + scale_ref[...] * proj[ROWS:2 * ROWS, :]).astype(BF16)

    for h in range(HEADS):
        q_copy(h).wait_send()
        part_copy(h).wait_send()
        stat_copy(h).wait_send()
        for i in range(TP - 1):
            att_copy(h, i).wait_send()
        for s in range(1, STEPS):
            for c in range(2):
                for d in range(2):
                    ring(h, s, d, c).wait_send()
        ring(h, STEPS, 0, 0).wait_send()
        ring(h, STEPS, 1, 1).wait_send()
    for i in range(TP - 1):
        w_copy(i).wait_send()


def per_device(q, qt, k, kt, v, vt, w, bias, scale, slope):
    vm = pl.BlockSpec(memory_space=pltpu.VMEM)
    dma = pltpu.SemaphoreType.DMA
    shape = jax.ShapeDtypeStruct((ROWS, COLS), BF16)
    return pl.pallas_call(
        kernel,
        out_shape=(shape, shape),
        in_specs=[vm] * 6 + [pl.BlockSpec(memory_space=pl.ANY)] + [vm] * 3,
        out_specs=(vm, vm),
        scratch_shapes=[
            pltpu.VMEM((HEADS, STEPS, 2 * ROWS, 4 * HD), BF16),
            pltpu.VMEM((HEADS, 2 * ROWS, 2 * HD), BF16),
            pltpu.VMEM((HEADS, TP * HD, COLS), BF16),
            pltpu.VMEM((HEADS, 2 * ROWS, TP * HD), BF16),
            pltpu.VMEM((2 * ROWS, COLS), F32),
            pltpu.VMEM((2 * ROWS, HD), F32),
            pltpu.VMEM((2 * ROWS, HD), F32),
            pltpu.VMEM((2 * ROWS, HD), F32),
            pltpu.VMEM((2 * ROWS, 2 * HD), F32),
            pltpu.VMEM((2 * ROWS, HD), F32),
            pltpu.VMEM((HEADS, ROWS, 2 * HD), F32),
            pltpu.VMEM((HEADS, 3, ROWS, HD), F32),
            pltpu.VMEM((HEADS, ROWS, 2 * HD), BF16),
            pltpu.VMEM((HEADS, ROWS, 2 * HD), BF16),
            pltpu.VMEM((HEADS, 8, HD), F32),
            pltpu.VMEM((HEADS, 8, HD), F32),
            dma((HEADS, STEPS, 2, 2)), dma((HEADS, STEPS, 2, 2)),
            dma((HEADS,)), dma((HEADS,)),
            dma((TP - 1,)), dma((TP - 1,)), dma,
            dma((HEADS,)), dma((HEADS,)), dma((HEADS,)), dma((HEADS,)),
            dma((HEADS, TP - 1)), dma((HEADS, TP - 1)),
        ],
        compiler_params=pltpu.CompilerParams(
            collective_id=0, has_side_effects=True, vmem_limit_bytes=48 * 2**20),
        name="attention",
    )(q, qt, k, kt, v, vt, w.reshape(HEADS, HD, -1), bias.reshape(1, -1),
      scale.reshape(1, -1), slope.reshape(1, -1))


def solution(mesh):
    in_specs = (
        P(("dp", "ctx"), "tp"),
        P(("dp", "ctx"), "tp"),
        P(("dp", "ctx"), "tp"),
        P(("dp", "ctx"), "tp"),
        P(("dp", "ctx"), "tp"),
        P(("dp", "ctx"), "tp"),
        P("tp", None),
        P("tp"),
        P(("dp", "tp")),
        P(("dp", "tp")),
    )
    out_specs = (P(("dp", "ctx"), "tp"), P(("dp", "ctx"), "tp"))
    return jax.shard_map(
        per_device, mesh=mesh, in_specs=in_specs, out_specs=out_specs, check_vma=False
    )
```

time: 584 us -> 131 us (0.22)
  waiting for transfers between devices: 434 us -> 0 us
  Pallas kernels: 0 us -> 119 us
  starting transfers between devices: 63.3 us -> 0 us
  matrix products: 52.2 us -> 0 us
  between operations: 14.2 us -> 0.65 us
    ppermute x31 -> x0, waiting for transfers between devices: 365 us -> none  [passed_along(): lax.ppermute(shard, axis, [(i, (i + by) % devices) for i in range(devices)])]
    pallas_call x0 -> x1, Pallas kernels: none -> 119 us  [per_device(): pl.pallas_call(kernel, out_shape=(shape, shape), in_specs=[vm] * 6 + [pl....]
    unnamed x2 -> x0, waiting for transfers between devices: 69.2 us -> none
    ppermute x31 -> x0, starting transfers between devices: 63.3 us -> none  [passed_along(): lax.ppermute(shard, axis, [(i, (i + by) % devices) for i in range(devices)])]
    dot_general x193 -> x0, matrix products: 52.2 us -> none  [the longest x32 8.35 us: absorb(): jnp.einsum('qhd,khd->qhk', local_query, keys, preferred_element_type=jnp....]
  transfers between devices with their start and end apart: 32 -> 0, of which waited for: 32 -> 0; matrix products, arithmetic and copies ran while one was open for 0% -> 0% of each run, Pallas kernels for 0% -> 0%
where the time goes in v1:
time: 131 us; the launch traced here: 130 us
  Pallas kernels  119 us (91%)
  local copies, waits for them, and re-layouts  10.9 us (8%)
    pallas_call x1, Pallas kernels, per_device(): pl.pallas_call(kernel, out_shape=(shape, shape), in_specs=[vm] * 6 + [pl....  119 us
    unnamed x16, local copies, waits for them, and re-layouts  8.8 us

profile of v1, /device:TPU:1, one launch (start us, length us, event | category | flops | bytes accessed | tf_op | source)
XLA Modules:
  0.0 130.3 jit_solution(4284653637964417999)
XLA Ops:
  0.6 0.7 reshape.17.bias_ref
  1.3 0.7 reshape.18.scale_ref
  2.0 0.7 reshape.19.slope_ref
  2.7 0.0 copy-start
  2.7 2.1 %copy-done = bf16[384,5120]{1,0:T(8,128)(2,1)S(1)} copy-done((bf16[384,5120]{1,0:T(8,128)(2,1)S(1)}, bf16[384,5120]{1,0:T(8,128)(2,1)}, u32[]{:S(2)}) %copy-start) | copy-done | bytes 3932184
  4.8 0.0 copy-start.1
  4.8 0.9 copy-done.1
  5.7 0.0 copy-start.2
  5.7 0.9 copy-done.2
  6.6 0.0 copy-start.3
  6.6 0.9 copy-done.3
  7.5 0.0 copy-start.4
  7.5 0.9 copy-done.4
  8.4 0.0 copy-start.5
  8.4 0.9 copy-done.5
  9.3 0.0 copy-start.6
  9.3 0.9 copy-done.6
  10.2 118.8 %attention.1 = (bf16[128,640]{1,0:T(8,128)(2,1)S(1)}, bf16[128,640]{1,0:T(8,128)(2,1)S(1)}) custom-call(bf16[128,384]{1,0:T(8,128)(2,1)S(1)} %copy-done.1, bf16[128,384]{1,0:T(8,128)(2,1)S(1)} %copy-done.2, bf16[128,384]{1,0:T(8,128)(2,1)S(1)} %copy-done.3, bf16[128,384]{1,0:T(8,128)(2,1)S(1)} %copy-done.4, bf16[128,384]{1,0:T(8,128)(2,1)S(1)} %copy-done.5, ...), custom_call_target="tpu_custom_call" | custom-call | tf_op jit(solution)/shard_map/attention/pallas_call | solution.py:285
  128.9 0.7 copy.14
  129.6 0.7 copy.15
Async XLA Ops:
  2.7 2.1 %copy-start = (bf16[384,5120]{1,0:T(8,128)(2,1)S(1)}, bf16[384,5120]{1,0:T(8,128)(2,1)}, u32[]{:S(2)}) copy-start(bf16[384,5120]{1,0:T(8,128)(2,1)} %param.16) | copy-start | bytes 11796484
  4.8 0.9 copy-start.1
  5.7 0.9 copy-start.2
  6.6 0.9 copy-start.3
  7.5 0.9 copy-start.4
  8.4 0.9 copy-start.5
  9.3 0.9 copy-start.6

commit v2 on v1

--- a/solution.py
+++ b/solution.py
@@ -13,6 +13,7 @@
 HALF = ROWS // 2
 RING = 16
 STEPS = RING // 2
+LAG = 2
 TP = 8
 COLS = 640
 FACTOR = HD ** (-0.5)
@@ -29,10 +30,10 @@
 def kernel(
     q_ref, qt_ref, k_ref, kt_ref, v_ref, vt_ref, w_ref, bias_ref, scale_ref, slope_ref,
     out_ref, outt_ref,
-    kv, qbuf, wbuf, att, proj, top, tot, slp, acc, acct,
+    bias, scale, slope, kv, qbuf, wbuf, att, proj, top, tot, slp, acc, acct,
     own_part, own_stat, part_out, part_in, stat_out, stat_in,
     ring_send, ring_recv, q_send, q_recv, w_send, w_recv, w_own,
-    part_ssem, part_rsem, stat_ssem, stat_rsem, att_send, att_recv,
+    part_ssem, part_rsem, stat_ssem, stat_rsem, att_send, att_recv, load_sem, gate_sem,
 ):
     ctx = lax.axis_index("ctx")
     tp = lax.axis_index("tp")
@@ -46,12 +47,23 @@
     for where in [{"ctx": right}, {"ctx": left}, {"ctx": partner}] + [{"tp": p} for p in peers]:
         pl.semaphore_signal(barrier, inc=1, device_id=where, device_id_type=MESH)
 
+    def load_copies(h):
+        cols = pl.ds(h * HD, HD)
+        targets = [(ref, kv.at[h, 0, pl.ds(0, ROWS), pl.ds(i * HD, HD)])
+                   for i, ref in enumerate((k_ref, kt_ref, v_ref, vt_ref))]
+        targets += [(ref, qbuf.at[h, pl.ds(0, ROWS), pl.ds(i * HD, HD)])
+                    for i, ref in enumerate((qt_ref, q_ref))]
+        return [pltpu.make_async_copy(ref.at[:, cols], target, load_sem.at[h, i])
+                for i, (ref, target) in enumerate(targets)]
+
+    gate_copies = [pltpu.make_async_copy(ref, target, gate_sem.at[i])
+                   for i, (ref, target) in enumerate(
+                       ((bias_ref, bias), (scale_ref, scale), (slope_ref, slope)))]
     for h in range(HEADS):
-        cols = slice(h * HD, (h + 1) * HD)
-        for i, ref in enumerate((k_ref, kt_ref, v_ref, vt_ref)):
-            kv[h, 0, 0:ROWS, i * HD:(i + 1) * HD] = ref[:, cols]
-        qbuf[h, 0:ROWS, 0:HD] = qt_ref[:, cols]
-        qbuf[h, 0:ROWS, HD:2 * HD] = q_ref[:, cols]
+        for copy in load_copies(h):
+            copy.start()
+    for copy in gate_copies:
+        copy.start()
 
     def ring(h, s, d, c):
         lo = c * HALF
@@ -111,8 +123,11 @@
         wbuf.at[:, pl.ds(pl.multiple_of(tp * HD, HD), HD), :], w_own)
 
     pl.semaphore_wait(barrier, 3 + TP - 1)
-    start_ring(0)
     for h in range(HEADS):
+        for copy in load_copies(h):
+            copy.wait()
+        if h == 0:
+            start_ring(0)
         q_copy(h).start()
     for i in range(TP - 1):
         w_copy(i).start()
@@ -128,10 +143,10 @@
         if first:
             new = jnp.broadcast_to(peak, (2 * ROWS, HD))
         else:
-            old = top[...]
+            old = top[h]
             new = jnp.maximum(old, peak)
             shrink = jnp.exp2((old - new) * EXP_SCALE)
-        top[...] = new
+        top[h] = new
         wide = jnp.concatenate([new] * (count // HD), axis=1) if count > HD else new
         weights = jnp.exp2((scores - wide) * EXP_SCALE)
         slanted = weights * tilt
@@ -143,33 +158,33 @@
         both = jnp.dot(weights.astype(BF16), values, preferred_element_type=F32)
         bent = jnp.dot(slanted.astype(BF16), values[:, :HD], preferred_element_type=F32)
         if first:
-            tot[...] = folded
-            slp[...] = tilted
-            acc[...] = both
-            acct[...] = bent
+            tot[h] = folded
+            slp[h] = tilted
+            acc[h] = both
+            acct[h] = bent
         else:
-            tot[...] = tot[...] * shrink + folded
-            slp[...] = slp[...] * shrink + tilted
-            acc[...] = acc[...] * jnp.concatenate([shrink, shrink], axis=1) + both
-            acct[...] = acct[...] * shrink + bent
+            tot[h] = tot[h] * shrink + folded
+            slp[h] = slp[h] * shrink + tilted
+            acc[h] = acc[h] * jnp.concatenate([shrink, shrink], axis=1) + both
+            acct[h] = acct[h] * shrink + bent
 
     def part_of(h):
-        total = jnp.sum(tot[...], axis=1, keepdims=True)
-        incline = jnp.sum(slp[...], axis=1, keepdims=True) * FACTOR
+        total = jnp.sum(tot[h], axis=1, keepdims=True)
+        incline = jnp.sum(slp[h], axis=1, keepdims=True) * FACTOR
         inverse = 1.0 / total
         incline = incline * inverse
-        main = acc[:, :HD] * inverse
-        tangent = (acct[...] * FACTOR + acc[:, HD:]) * inverse - main * incline
+        main = acc[h, :, :HD] * inverse
+        tangent = (acct[h] * FACTOR + acc[h, :, HD:]) * inverse - main * incline
         own_part[h, :, :HD] = main[:ROWS]
         own_part[h, :, HD:] = tangent[:ROWS]
         part_out[h, :, :HD] = main[ROWS:].astype(BF16)
         part_out[h, :, HD:] = tangent[ROWS:].astype(BF16)
         part_copy(h).start()
         lane = lax.broadcasted_iota(jnp.int32, (ROWS, HD), 1)
-        stat = jnp.where(lane == 0, top[ROWS:, :], jnp.where(lane == 1, total[ROWS:], incline[ROWS:]))
+        stat = jnp.where(lane == 0, top[h, ROWS:, :], jnp.where(lane == 1, total[ROWS:], incline[ROWS:]))
         stat_out[h] = stat.T[0:8]
         stat_copy(h).start()
-        own_stat[h, 0] = top[0:ROWS, :]
+        own_stat[h, 0] = top[h, 0:ROWS, :]
         own_stat[h, 1] = jnp.broadcast_to(total[:ROWS], (ROWS, HD))
         own_stat[h, 2] = jnp.broadcast_to(incline[:ROWS], (ROWS, HD))
 
@@ -217,50 +232,74 @@
                 if (c, d) in sends:
                     ring(h, s + 1, d, c).start()
 
+    def slot(k, attending):
+        def at(h):
+            return k - h * LAG
+
+        if not isinstance(k, int):
+            for h in range(1, HEADS - 1):
+                pl.when(k == STEPS + (h + 1) * LAG)(lambda h=h: join(h))
+        for h in range(HEADS):
+            s = at(h)
+            if isinstance(k, int):
+                if 1 <= s < STEPS - 1:
+                    pass_on(h, s)
+            else:
+                pl.when((s >= 2) & (s < STEPS - 1))(lambda h=h, s=s: pass_on(h, s))
+                pl.when(s == 1)(lambda h=h: pass_on(h, 1))
+                pl.when(s == STEPS - 1)(lambda h=h: pass_on(h, STEPS - 1, ((0, 0), (1, 1))))
+            if h > 0:
+                if isinstance(k, int):
+                    if s == 0:
+                        start_ring(h)
+                else:
+                    pl.when(s == 0)(lambda h=h: start_ring(h))
+        if not attending:
+            return
+        for h in range(HEADS):
+            s = at(h)
+
+            def inner(h=h, s=s):
+                pl.when(s == 1)(lambda: attend(h, kv.at[h, 0, pl.ds(0, ROWS)], first=True))
+                attend(h, kv.at[h, s])
+
+            def last(h=h):
+                ring(h, STEPS, 0, 0).wait_recv()
+                ring(h, STEPS, 1, 1).wait_recv()
+                attend(h, kv.at[h, 0, pl.ds(ROWS, ROWS)])
+                part_of(h)
+
+            pl.when((s >= 1) & (s < STEPS))(inner)
+            pl.when(s == STEPS)(last)
+        pl.when(k == STEPS + LAG)(lambda: join(0))
+
+    for k in range(1, 3):
+        slot(k, False)
+    for i in range(HEADS):
+        q_copy(i).wait_recv()
     for h in range(HEADS):
-        if h == 0:
-            pass_on(0, 1)
-            pass_on(0, 2)
-            for i in range(HEADS):
-                q_copy(i).wait_recv()
-            attend(0, kv.at[0, 0, pl.ds(0, ROWS)], first=True)
-            attend(0, kv.at[0, 1])
-            attend(0, kv.at[0, 2])
-            begin = 3
-        else:
+        if 2 - h * LAG >= 1:
             attend(h, kv.at[h, 0, pl.ds(0, ROWS)], first=True)
-            begin = 1
-
-        def turn(s, carry, h=h):
-            pass_on(h, s)
+        for s in range(1, 3 - h * LAG):
             attend(h, kv.at[h, s])
-            return carry
-
-        if begin == 1:
-            pass_on(h, 1)
-            attend(h, kv.at[h, 1])
-            begin = 2
-        lax.fori_loop(begin, 4, turn, 0)
-        if h > 0:
-            join(h - 1)
-        lax.fori_loop(4, STEPS - 1, turn, 0)
-        pass_on(h, STEPS - 1, sends=((0, 0), (1, 1)))
-        if h + 1 < HEADS:
-            start_ring(h + 1)
-        attend(h, kv.at[h, STEPS - 1])
-        ring(h, STEPS, 0, 0).wait_recv()
-        ring(h, STEPS, 1, 1).wait_recv()
-        attend(h, kv.at[h, 0, pl.ds(ROWS, ROWS)])
-        part_of(h)
+
+    def turn(k, carry):
+        slot(k, True)
+        return carry
+
+    lax.fori_loop(3, STEPS + (HEADS - 1) * LAG + 1, turn, 0)
 
     project(0)
     project(1)
     join(HEADS - 1)
     project(HEADS - 1)
 
-    shifted = proj[0:ROWS, :] + bias_ref[...]
-    out_ref[...] = (scale_ref[...] * shifted).astype(BF16)
-    outt_ref[...] = (slope_ref[...] * shifted + scale_ref[...] * proj[ROWS:2 * ROWS, :]).astype(BF16)
+    for copy in gate_copies:
+        copy.wait()
+    gate, gate_dot = scale[...].reshape(1, COLS), slope[...].reshape(1, COLS)
+    shifted = proj[0:ROWS, :] + bias[...].reshape(1, COLS)
+    out_ref[...] = (gate * shifted).astype(BF16)
+    outt_ref[...] = (gate_dot * shifted + gate * proj[ROWS:2 * ROWS, :]).astype(BF16)
 
     for h in range(HEADS):
         q_copy(h).wait_send()
@@ -285,19 +324,20 @@
     return pl.pallas_call(
         kernel,
         out_shape=(shape, shape),
-        in_specs=[vm] * 6 + [pl.BlockSpec(memory_space=pl.ANY)] + [vm] * 3,
+        in_specs=[pl.BlockSpec(memory_space=pl.ANY)] * 10,
         out_specs=(vm, vm),
         scratch_shapes=[
+            pltpu.VMEM((COLS,), F32), pltpu.VMEM((COLS,), F32), pltpu.VMEM((COLS,), F32),
             pltpu.VMEM((HEADS, STEPS, 2 * ROWS, 4 * HD), BF16),
             pltpu.VMEM((HEADS, 2 * ROWS, 2 * HD), BF16),
             pltpu.VMEM((HEADS, TP * HD, COLS), BF16),
             pltpu.VMEM((HEADS, 2 * ROWS, TP * HD), BF16),
             pltpu.VMEM((2 * ROWS, COLS), F32),
-            pltpu.VMEM((2 * ROWS, HD), F32),
-            pltpu.VMEM((2 * ROWS, HD), F32),
-            pltpu.VMEM((2 * ROWS, HD), F32),
-            pltpu.VMEM((2 * ROWS, 2 * HD), F32),
-            pltpu.VMEM((2 * ROWS, HD), F32),
+            pltpu.VMEM((HEADS, 2 * ROWS, HD), F32),
+            pltpu.VMEM((HEADS, 2 * ROWS, HD), F32),
+            pltpu.VMEM((HEADS, 2 * ROWS, HD), F32),
+            pltpu.VMEM((HEADS, 2 * ROWS, 2 * HD), F32),
+            pltpu.VMEM((HEADS, 2 * ROWS, HD), F32),
             pltpu.VMEM((HEADS, ROWS, 2 * HD), F32),
             pltpu.VMEM((HEADS, 3, ROWS, HD), F32),
             pltpu.VMEM((HEADS, ROWS, 2 * HD), BF16),
@@ -308,13 +348,12 @@
             dma((HEADS,)), dma((HEADS,)),
             dma((TP - 1,)), dma((TP - 1,)), dma,
             dma((HEADS,)), dma((HEADS,)), dma((HEADS,)), dma((HEADS,)),
-            dma((HEADS, TP - 1)), dma((HEADS, TP - 1)),
+            dma((HEADS, TP - 1)), dma((HEADS, TP - 1)), dma((HEADS, 6)), dma((3,)),
         ],
         compiler_params=pltpu.CompilerParams(
-            collective_id=0, has_side_effects=True, vmem_limit_bytes=48 * 2**20),
+            collective_id=0, has_side_effects=True, vmem_limit_bytes=63 * 2**20),
         name="attention",
-    )(q, qt, k, kt, v, vt, w.reshape(HEADS, HD, -1), bias.reshape(1, -1),
-      scale.reshape(1, -1), slope.reshape(1, -1))
+    )(q, qt, k, kt, v, vt, w.reshape(HEADS, HD, -1), bias, scale, slope)
 
 
 def solution(mesh):

time: 131 us -> 107 us (0.82)
  Pallas kernels: 119 us -> 103 us
  local copies, waits for them, and re-layouts: 10.9 us -> 3.19 us
    pallas_call x1, Pallas kernels: 119 us -> 103 us  [per_device(): pl.pallas_call(kernel, out_shape=(shape, shape), in_specs=[pl.BlockSpec(m...]
    unnamed x16 -> x2, local copies, waits for them, and re-layouts: 8.8 us -> 3.19 us
    reshape x3 -> x0, local copies, waits for them, and re-layouts: 2.07 us -> none  [the longest x1 0.69 us: per_device(): bias.reshape(1, -1)]
where the time goes in v2:
time: 107 us; the launch traced here: 106 us
  Pallas kernels  103 us (96%)
  local copies, waits for them, and re-layouts  3.19 us (3%)
    pallas_call x1, Pallas kernels, per_device(): pl.pallas_call(kernel, out_shape=(shape, shape), in_specs=[pl.BlockSpec(m...  103 us
    unnamed x2, local copies, waits for them, and re-layouts  3.19 us

profile of v2, /device:TPU:1, one launch (start us, length us, event | category | flops | bytes accessed | tf_op | source)
XLA Modules:
  0.0 106.3 jit_solution(12739444029838025589)
XLA Ops:
  0.6 102.5 %attention.1 = (bf16[128,640]{1,0:T(8,128)(2,1)}, bf16[128,640]{1,0:T(8,128)(2,1)}) custom-call(bf16[128,384]{1,0:T(8,128)(2,1)} %q_ref.1, bf16[128,384]{1,0:T(8,128)(2,1)} %qt_ref.1, bf16[128,384]{1,0:T(8,128)(2,1)} %k_ref.1, bf16[128,384]{1,0:T(8,128)(2,1)} %kt_ref.1, bf16[128,384]{1,0:T(8,128)(2,1)} %v_ref.1, bf16[128,384]{1,0:T(8,128)(2,1)} %vt_ref.1, ...), custom_call_target="tpu_custom_call" | custom-call | tf_op jit(solution)/shard_map/attention/pallas_call | solution.py:324
  103.1 1.6 %copy.14 = bf16[128,640]{1,0:T(8,128)(2,1)} copy(bf16[128,640]{1,0:T(8,128)(2,1)} %get-tuple-element.4) | data formatting | bytes 327680
  104.7 1.6 %copy.15 = bf16[128,640]{1,0:T(8,128)(2,1)} copy(bf16[128,640]{1,0:T(8,128)(2,1)} %get-tuple-element.5) | data formatting | bytes 327680

commit v3 on v2

--- a/solution.py
+++ b/solution.py
@@ -13,8 +13,10 @@
 HALF = ROWS // 2
 RING = 16
 STEPS = RING // 2
-LAG = 2
+OFFSET = (0, 2, 4)
+START = (0, 0, 2)
 TP = 8
+CHIPS = TP // 2 - 1
 COLS = 640
 FACTOR = HD ** (-0.5)
 EXP_SCALE = FACTOR * math.log2(math.e)
@@ -28,23 +30,25 @@
 
 
 def kernel(
-    q_ref, qt_ref, k_ref, kt_ref, v_ref, vt_ref, w_ref, bias_ref, scale_ref, slope_ref,
-    out_ref, outt_ref,
-    bias, scale, slope, kv, qbuf, wbuf, att, proj, top, tot, slp, acc, acct,
+    q_ref, qt_ref, k_ref, kt_ref, v_ref, vt_ref, w_ref, out_ref,
+    kv, qbuf, wbuf, att, proj, top, tot, slp, acc, acct,
     own_part, own_stat, part_out, part_in, stat_out, stat_in,
     ring_send, ring_recv, q_send, q_recv, w_send, w_recv, w_own,
-    part_ssem, part_rsem, stat_ssem, stat_rsem, att_send, att_recv, load_sem, gate_sem,
+    part_ssem, part_rsem, stat_ssem, stat_rsem, att_send, att_recv, load_sem,
 ):
     ctx = lax.axis_index("ctx")
     tp = lax.axis_index("tp")
     z, y = ctx // 2, ctx % 2
     right = lax.rem(z + 1, RING) * 2 + y
     left = lax.rem(z + RING - 1, RING) * 2 + y
+    far_right = lax.rem(z + 2, RING) * 2 + y
+    far_left = lax.rem(z + RING - 2, RING) * 2 + y
     partner = z * 2 + (1 - y)
+    sibling = tp + 1 - 2 * lax.rem(tp, 2)
     peers = [lax.rem(tp + i, TP) for i in range(1, TP)]
 
     barrier = pltpu.get_barrier_semaphore()
-    for where in [{"ctx": right}, {"ctx": left}, {"ctx": partner}] + [{"tp": p} for p in peers]:
+    for where in [{"ctx": c} for c in (right, left, far_right, far_left, partner)] + [{"tp": p} for p in peers]:
         pl.semaphore_signal(barrier, inc=1, device_id=where, device_id_type=MESH)
 
     def load_copies(h):
@@ -56,19 +60,18 @@
         return [pltpu.make_async_copy(ref.at[:, cols], target, load_sem.at[h, i])
                 for i, (ref, target) in enumerate(targets)]
 
-    gate_copies = [pltpu.make_async_copy(ref, target, gate_sem.at[i])
-                   for i, (ref, target) in enumerate(
-                       ((bias_ref, bias), (scale_ref, scale), (slope_ref, slope)))]
     for h in range(HEADS):
         for copy in load_copies(h):
             copy.start()
-    for copy in gate_copies:
-        copy.start()
 
     def ring(h, s, d, c):
         lo = c * HALF
+        targets = (right, left)
         if isinstance(s, int) and s == STEPS:
-            src = kv.at[h, STEPS - 1, pl.ds(d * ROWS + lo, HALF)]
+            back = 1
+            if h == HEADS - 1:
+                back, targets = 2, (far_right, far_left)
+            src = kv.at[h, STEPS - back, pl.ds(d * ROWS + lo, HALF)]
             dst = kv.at[h, 0, pl.ds(ROWS + lo, HALF)]
         else:
             first = isinstance(s, int) and s == 1
@@ -77,7 +80,7 @@
         return pltpu.make_async_remote_copy(
             src_ref=src, dst_ref=dst,
             send_sem=ring_send.at[h, s - 1, d, c], recv_sem=ring_recv.at[h, s - 1, d, c],
-            device_id={"ctx": right if d == 0 else left}, device_id_type=MESH)
+            device_id={"ctx": targets[d]}, device_id_type=MESH)
 
     def start_ring(h):
         for c in range(2):
@@ -99,12 +102,18 @@
             device_id={"tp": peer}, device_id_type=MESH)
 
     def att_copy(h, i):
-        peer = lax.rem(tp + i + 1, TP)
-        mine = att.at[h, :, pl.ds(pl.multiple_of(tp * HD, HD), HD)]
-        return pltpu.make_async_remote_copy(
-            src_ref=mine, dst_ref=mine,
+        owner = tp if i <= CHIPS else lax.rem(tp + TP - 2 * (i - CHIPS), TP)
+        peer = lax.rem(tp + 2 * (i + 1), TP) if i < CHIPS else sibling
+        part = att.at[h, :, pl.ds(pl.multiple_of(owner * HD, HD), HD)]
+        return pltpu.make_async_remote_copy(
+            src_ref=part, dst_ref=part,
             send_sem=att_send.at[h, i], recv_sem=att_recv.at[h, i],
             device_id={"tp": peer}, device_id_type=MESH)
+
+    def relay(h):
+        for i in range(CHIPS):
+            att_copy(h, i).wait_recv()
+            att_copy(h, CHIPS + 1 + i).start()
 
     def part_copy(h):
         return pltpu.make_async_remote_copy(
@@ -122,12 +131,13 @@
         w_ref.at[:, :, pl.ds(pl.multiple_of(tp * COLS, COLS), COLS)],
         wbuf.at[:, pl.ds(pl.multiple_of(tp * HD, HD), HD), :], w_own)
 
-    pl.semaphore_wait(barrier, 3 + TP - 1)
+    pl.semaphore_wait(barrier, 5 + TP - 1)
     for h in range(HEADS):
         for copy in load_copies(h):
             copy.wait()
-        if h == 0:
-            start_ring(0)
+        if START[h] == 0:
+            start_ring(h)
+    for h in range(HEADS):
         q_copy(h).start()
     for i in range(TP - 1):
         w_copy(i).start()
@@ -209,11 +219,11 @@
         cols = pl.ds(pl.multiple_of(tp * HD, HD), HD)
         att[h, 0:ROWS, cols] = main.astype(BF16)
         att[h, ROWS:2 * ROWS, cols] = tangent.astype(BF16)
-        for i in range(TP - 1):
+        for i in range(CHIPS + 1):
             att_copy(h, i).start()
 
     def project(h):
-        for i in range(TP - 1):
+        for i in range(CHIPS, TP - 1):
             att_copy(h, i).wait_recv()
         if h == 0:
             own_w.wait()
@@ -222,8 +232,10 @@
         term = jnp.dot(att[h], wbuf[h], preferred_element_type=F32)
         if h == 0:
             proj[...] = term
+        elif h < HEADS - 1:
+            proj[...] += term
         else:
-            proj[...] += term
+            out_ref[...] = proj[...] + term
 
     def pass_on(h, s, sends=((0, 0), (0, 1), (1, 0), (1, 1))):
         for c in range(2):
@@ -234,11 +246,8 @@
 
     def slot(k, attending):
         def at(h):
-            return k - h * LAG
-
-        if not isinstance(k, int):
-            for h in range(1, HEADS - 1):
-                pl.when(k == STEPS + (h + 1) * LAG)(lambda h=h: join(h))
+            return k - OFFSET[h]
+
         for h in range(HEADS):
             s = at(h)
             if isinstance(k, int):
@@ -247,13 +256,17 @@
             else:
                 pl.when((s >= 2) & (s < STEPS - 1))(lambda h=h, s=s: pass_on(h, s))
                 pl.when(s == 1)(lambda h=h: pass_on(h, 1))
-                pl.when(s == STEPS - 1)(lambda h=h: pass_on(h, STEPS - 1, ((0, 0), (1, 1))))
-            if h > 0:
+                if h < HEADS - 1:
+                    pl.when(s == STEPS - 1)(lambda h=h: pass_on(h, STEPS - 1, ((0, 0), (1, 1))))
+                else:
+                    pl.when(s == STEPS - 2)(lambda h=h: [ring(h, STEPS, d, d).start() for d in range(2)] and None)
+                    pl.when(s == STEPS - 1)(lambda h=h: pass_on(h, STEPS - 1, ()))
+            if START[h] > 0:
                 if isinstance(k, int):
-                    if s == 0:
+                    if k == START[h]:
                         start_ring(h)
                 else:
-                    pl.when(s == 0)(lambda h=h: start_ring(h))
+                    pl.when(k == START[h])(lambda h=h: start_ring(h))
         if not attending:
             return
         for h in range(HEADS):
@@ -271,35 +284,32 @@
 
             pl.when((s >= 1) & (s < STEPS))(inner)
             pl.when(s == STEPS)(last)
-        pl.when(k == STEPS + LAG)(lambda: join(0))
+        pl.when(k == STEPS + 2)(lambda: relay(0))
+        for h in range(HEADS - 1):
+            pl.when(k == STEPS + OFFSET[h] + 1)(lambda h=h: join(h))
 
     for k in range(1, 3):
         slot(k, False)
     for i in range(HEADS):
         q_copy(i).wait_recv()
     for h in range(HEADS):
-        if 2 - h * LAG >= 1:
+        if 2 - OFFSET[h] >= 1:
             attend(h, kv.at[h, 0, pl.ds(0, ROWS)], first=True)
-        for s in range(1, 3 - h * LAG):
+        for s in range(1, 3 - OFFSET[h]):
             attend(h, kv.at[h, s])
 
     def turn(k, carry):
         slot(k, True)
         return carry
 
-    lax.fori_loop(3, STEPS + (HEADS - 1) * LAG + 1, turn, 0)
+    lax.fori_loop(3, STEPS + OFFSET[-1] + 1, turn, 0)
 
     project(0)
+    relay(1)
+    join(2)
     project(1)
-    join(HEADS - 1)
-    project(HEADS - 1)
-
-    for copy in gate_copies:
-        copy.wait()
-    gate, gate_dot = scale[...].reshape(1, COLS), slope[...].reshape(1, COLS)
-    shifted = proj[0:ROWS, :] + bias[...].reshape(1, COLS)
-    out_ref[...] = (gate * shifted).astype(BF16)
-    outt_ref[...] = (gate_dot * shifted + gate * proj[ROWS:2 * ROWS, :]).astype(BF16)
+    relay(2)
+    project(2)
 
     for h in range(HEADS):
         q_copy(h).wait_send()
@@ -320,14 +330,12 @@
 def per_device(q, qt, k, kt, v, vt, w, bias, scale, slope):
     vm = pl.BlockSpec(memory_space=pltpu.VMEM)
     dma = pltpu.SemaphoreType.DMA
-    shape = jax.ShapeDtypeStruct((ROWS, COLS), BF16)
-    return pl.pallas_call(
+    proj = pl.pallas_call(
         kernel,
-        out_shape=(shape, shape),
-        in_specs=[pl.BlockSpec(memory_space=pl.ANY)] * 10,
-        out_specs=(vm, vm),
+        out_shape=jax.ShapeDtypeStruct((2 * ROWS, COLS), F32),
+        in_specs=[pl.BlockSpec(memory_space=pl.ANY)] * 7,
+        out_specs=vm,
         scratch_shapes=[
-            pltpu.VMEM((COLS,), F32), pltpu.VMEM((COLS,), F32), pltpu.VMEM((COLS,), F32),
             pltpu.VMEM((HEADS, STEPS, 2 * ROWS, 4 * HD), BF16),
             pltpu.VMEM((HEADS, 2 * ROWS, 2 * HD), BF16),
             pltpu.VMEM((HEADS, TP * HD, COLS), BF16),
@@ -348,12 +356,16 @@
             dma((HEADS,)), dma((HEADS,)),
             dma((TP - 1,)), dma((TP - 1,)), dma,
             dma((HEADS,)), dma((HEADS,)), dma((HEADS,)), dma((HEADS,)),
-            dma((HEADS, TP - 1)), dma((HEADS, TP - 1)), dma((HEADS, 6)), dma((3,)),
+            dma((HEADS, TP - 1)), dma((HEADS, TP - 1)), dma((HEADS, 6)),
         ],
         compiler_params=pltpu.CompilerParams(
             collective_id=0, has_side_effects=True, vmem_limit_bytes=63 * 2**20),
         name="attention",
-    )(q, qt, k, kt, v, vt, w.reshape(HEADS, HD, -1), bias, scale, slope)
+    )(q, qt, k, kt, v, vt, w.reshape(HEADS, HD, -1))
+    shifted = proj[:ROWS] + bias[None, :]
+    block_output = (scale[None, :] * shifted).astype(BF16)
+    output_tangent = (slope[None, :] * shifted + scale[None, :] * proj[ROWS:]).astype(BF16)
+    return block_output, output_tangent
 
 
 def solution(mesh):

time: 107 us -> 101 us (0.944)
  Pallas kernels: 103 us -> 98 us
  local copies, waits for them, and re-layouts: 3.19 us -> 0.01 us
  other arithmetic: 0 us -> 1.87 us
    pallas_call x1, Pallas kernels: 103 us -> 98 us  [per_device(): pl.pallas_call(kernel, out_shape=jax.ShapeDtypeStruct((2 * ROWS, COLS), F...]
    unnamed x2 -> x6, local copies, waits for them, and re-layouts: 3.19 us -> 0.01 us
    convert_element_type x0 -> x1, other arithmetic: none -> 1.87 us  [per_device(): (slope[None, :] * shifted + scale[None, :] * proj[ROWS:]).astype(BF16)]
where the time goes in v3:
time: 101 us
  Pallas kernels  98 us (97%)
  other arithmetic  1.87 us (2%)
    pallas_call x1, Pallas kernels, per_device(): pl.pallas_call(kernel, out_shape=jax.ShapeDtypeStruct((2 * ROWS, COLS), F...  98 us

profile of v3, /device:TPU:1, one launch (start us, length us, event | category | flops | bytes accessed | tf_op | source)
XLA Modules:
  0.0 100.5 jit_solution(6590144838984633965)
XLA Ops:
  0.6 0.0 copy-start
  0.6 0.0 copy-start.2
  0.7 0.0 copy-start.1
  0.7 98.0 %attention.1 = f32[256,640]{1,0:T(8,128)} custom-call(bf16[128,384]{1,0:T(8,128)(2,1)} %q_ref.1, bf16[128,384]{1,0:T(8,128)(2,1)} %qt_ref.1, bf16[128,384]{1,0:T(8,128)(2,1)} %k_ref.1, bf16[128,384]{1,0:T(8,128)(2,1)} %kt_ref.1, bf16[128,384]{1,0:T(8,128)(2,1)} %v_ref.1, bf16[128,384]{1,0:T(8,128)(2,1)} %vt_ref.1, bf16[3,128,5120]{2,1,0:T(8,128)(2,1)} %bitcast.1), custom_call_target="tpu_custom_call" | custom-call | tf_op jit(solution)/shard_map/attention/pallas_call | solution.py:333
  98.6 0.0 copy-done
  98.6 0.0 copy-done.2
  98.7 0.0 copy-done.1
  98.7 1.9 %add_convert_fusion = (bf16[128,640]{1,0:T(8,128)(2,1)}, bf16[128,640]{1,0:T(8,128)(2,1)}) fusion(f32[256,640]{1,0:T(8,128)} %attention.1, f32[640]{0:T(1024)S(1)} %copy-done, f32[640]{0:T(1024)S(1)} %copy-done.1, f32[640]{0:T(1024)S(1)} %copy-done.2), kind=kLoop, calls=%fused_computation | loop fusion | flops 573440 | bytes 990720 | tf_op jit(solution)/shard_map/convert_element_type | solution.py:367
Async XLA Ops:
  0.6 98.0 %copy-start = (f32[640]{0:T(1024)S(1)}, f32[640]{0:T(1024)}, u32[]{:S(2)}) copy-start(f32[640]{0:T(1024)} %param.19) | copy-start | bytes 7684
  0.6 98.0 %copy-start.2 = (f32[640]{0:T(1024)S(1)}, f32[640]{0:T(1024)}, u32[]{:S(2)}) copy-start(f32[640]{0:T(1024)} %param.18) | copy-start | bytes 7684
  0.7 98.0 %copy-start.1 = (f32[640]{0:T(1024)S(1)}, f32[640]{0:T(1024)}, u32[]{:S(2)}) copy-start(f32[640]{0:T(1024)} %param.17) | copy-start | bytes 7684

commit v4 on v3

--- a/solution.py
+++ b/solution.py
@@ -101,24 +101,26 @@
             send_sem=w_send.at[i], recv_sem=w_recv.at[i],
             device_id={"tp": peer}, device_id_type=MESH)
 
-    def att_copy(h, i):
+    def att_copy(h, r, i):
         owner = tp if i <= CHIPS else lax.rem(tp + TP - 2 * (i - CHIPS), TP)
         peer = lax.rem(tp + 2 * (i + 1), TP) if i < CHIPS else sibling
-        part = att.at[h, :, pl.ds(pl.multiple_of(owner * HD, HD), HD)]
+        part = att.at[h, pl.ds(r * ROWS, ROWS), pl.ds(pl.multiple_of(owner * HD, HD), HD)]
         return pltpu.make_async_remote_copy(
             src_ref=part, dst_ref=part,
-            send_sem=att_send.at[h, i], recv_sem=att_recv.at[h, i],
+            send_sem=att_send.at[h, r, i], recv_sem=att_recv.at[h, r, i],
             device_id={"tp": peer}, device_id_type=MESH)
 
     def relay(h):
-        for i in range(CHIPS):
-            att_copy(h, i).wait_recv()
-            att_copy(h, CHIPS + 1 + i).start()
-
-    def part_copy(h):
-        return pltpu.make_async_remote_copy(
-            src_ref=part_out.at[h], dst_ref=part_in.at[h],
-            send_sem=part_ssem.at[h], recv_sem=part_rsem.at[h],
+        for r in range(2):
+            for i in (0, 2, 1):
+                att_copy(h, r, i).wait_recv()
+                att_copy(h, r, CHIPS + 1 + i).start()
+
+    def part_copy(h, r):
+        rows = pl.ds(r * HALF, HALF)
+        return pltpu.make_async_remote_copy(
+            src_ref=part_out.at[h, rows], dst_ref=part_in.at[h, rows],
+            send_sem=part_ssem.at[h, r], recv_sem=part_rsem.at[h, r],
             device_id={"ctx": partner}, device_id_type=MESH)
 
     def stat_copy(h):
@@ -180,27 +182,33 @@
 
     def part_of(h):
         total = jnp.sum(tot[h], axis=1, keepdims=True)
-        incline = jnp.sum(slp[h], axis=1, keepdims=True) * FACTOR
         inverse = 1.0 / total
-        incline = incline * inverse
-        main = acc[h, :, :HD] * inverse
-        tangent = (acct[h] * FACTOR + acc[h, :, HD:]) * inverse - main * incline
-        own_part[h, :, :HD] = main[:ROWS]
-        own_part[h, :, HD:] = tangent[:ROWS]
-        part_out[h, :, :HD] = main[ROWS:].astype(BF16)
-        part_out[h, :, HD:] = tangent[ROWS:].astype(BF16)
-        part_copy(h).start()
+        incline = jnp.sum(slp[h], axis=1, keepdims=True) * FACTOR * inverse
         lane = lax.broadcasted_iota(jnp.int32, (ROWS, HD), 1)
         stat = jnp.where(lane == 0, top[h, ROWS:, :], jnp.where(lane == 1, total[ROWS:], incline[ROWS:]))
         stat_out[h] = stat.T[0:8]
         stat_copy(h).start()
+
+        def piece(rows):
+            main = acc[h, rows, :HD] * inverse[rows]
+            tangent = (acct[h, rows] * FACTOR + acc[h, rows, HD:]) * inverse[rows] - main * incline[rows]
+            return main, tangent
+
+        for r in range(2):
+            rows = slice(r * HALF, (r + 1) * HALF)
+            main, tangent = piece(slice(ROWS + r * HALF, ROWS + (r + 1) * HALF))
+            part_out[h, rows, :HD] = main.astype(BF16)
+            part_out[h, rows, HD:] = tangent.astype(BF16)
+            part_copy(h, r).start()
+        main, tangent = piece(slice(0, ROWS))
+        own_part[h, :, :HD] = main
+        own_part[h, :, HD:] = tangent
         own_stat[h, 0] = top[h, 0:ROWS, :]
         own_stat[h, 1] = jnp.broadcast_to(total[:ROWS], (ROWS, HD))
         own_stat[h, 2] = jnp.broadcast_to(incline[:ROWS], (ROWS, HD))
 
     def join(h):
         stat_copy(h).wait_recv()
-        part_copy(h).wait_recv()
         theirs = jnp.concatenate([stat_in[h]] * (HD // 8), axis=0).T
         top1, total1, incline1 = theirs[:, 0:1], theirs[:, 1:2], theirs[:, 2:3]
         top0, total0, incline0 = own_stat[h, 0], own_stat[h, 1], own_stat[h, 2]
@@ -211,31 +219,39 @@
         share0 = share0 * inverse
         share1 = share1 * inverse
         incline = share0 * incline0 + share1 * incline1
-        main0, tan0 = own_part[h, :, :HD], own_part[h, :, HD:]
-        main1, tan1 = part_in[h, :, :HD].astype(F32), part_in[h, :, HD:].astype(F32)
-        main = share0 * main0 + share1 * main1
-        tangent = (share0 * (tan0 + main0 * (incline0 - incline))
-                   + share1 * (tan1 + main1 * (incline1 - incline)))
         cols = pl.ds(pl.multiple_of(tp * HD, HD), HD)
-        att[h, 0:ROWS, cols] = main.astype(BF16)
-        att[h, ROWS:2 * ROWS, cols] = tangent.astype(BF16)
-        for i in range(CHIPS + 1):
-            att_copy(h, i).start()
+        for r in range(2):
+            rows = slice(r * HALF, (r + 1) * HALF)
+            part_copy(h, r).wait_recv()
+            main0, tan0 = own_part[h, rows, :HD], own_part[h, rows, HD:]
+            main1, tan1 = part_in[h, rows, :HD].astype(F32), part_in[h, rows, HD:].astype(F32)
+            part0, part1, tilt = share0[rows], share1[rows], incline[rows]
+            main = part0 * main0 + part1 * main1
+            tangent = (part0 * (tan0 + main0 * (incline0[rows] - tilt))
+                       + part1 * (tan1 + main1 * (incline1[rows] - tilt)))
+            att[h, r * ROWS:r * ROWS + HALF, cols] = main.astype(BF16)
+            att[h, r * ROWS + HALF:(r + 1) * ROWS, cols] = tangent.astype(BF16)
+            for i in (1, 0, 2, CHIPS):
+                att_copy(h, r, i).start()
 
     def project(h):
-        for i in range(CHIPS, TP - 1):
-            att_copy(h, i).wait_recv()
         if h == 0:
             own_w.wait()
             for i in range(TP - 1):
                 w_copy(i).wait_recv()
-        term = jnp.dot(att[h], wbuf[h], preferred_element_type=F32)
-        if h == 0:
-            proj[...] = term
-        elif h < HEADS - 1:
-            proj[...] += term
-        else:
-            out_ref[...] = proj[...] + term
+        for r in range(2):
+            rows = slice(r * ROWS, (r + 1) * ROWS)
+            for i in range(CHIPS, TP - 1):
+                att_copy(h, r, i).wait_recv()
+            term = jnp.dot(att[h, rows], wbuf[h], preferred_element_type=F32)
+            if h == 0:
+                proj[rows] = term
+            elif h < HEADS - 1:
+                proj[rows] += term
+            else:
+                term = proj[rows] + term
+                out_ref[r * HALF:(r + 1) * HALF] = term[:HALF]
+                out_ref[ROWS + r * HALF:ROWS + (r + 1) * HALF] = term[HALF:]
 
     def pass_on(h, s, sends=((0, 0), (0, 1), (1, 0), (1, 1))):
         for c in range(2):
@@ -306,17 +322,11 @@
 
     project(0)
     relay(1)
-    join(2)
-    project(1)
-    relay(2)
-    project(2)
-
     for h in range(HEADS):
         q_copy(h).wait_send()
-        part_copy(h).wait_send()
+        for r in range(2):
+            part_copy(h, r).wait_send()
         stat_copy(h).wait_send()
-        for i in range(TP - 1):
-            att_copy(h, i).wait_send()
         for s in range(1, STEPS):
             for c in range(2):
                 for d in range(2):
@@ -325,6 +335,15 @@
         ring(h, STEPS, 1, 1).wait_send()
     for i in range(TP - 1):
         w_copy(i).wait_send()
+    join(2)
+    project(1)
+    relay(2)
+    project(2)
+
+    for h in range(HEADS):
+        for r in range(2):
+            for i in range(TP - 1):
+                att_copy(h, r, i).wait_send()
 
 
 def per_device(q, qt, k, kt, v, vt, w, bias, scale, slope):
@@ -355,8 +374,8 @@
             dma((HEADS, STEPS, 2, 2)), dma((HEADS, STEPS, 2, 2)),
             dma((HEADS,)), dma((HEADS,)),
             dma((TP - 1,)), dma((TP - 1,)), dma,
-            dma((HEADS,)), dma((HEADS,)), dma((HEADS,)), dma((HEADS,)),
-            dma((HEADS, TP - 1)), dma((HEADS, TP - 1)), dma((HEADS, 6)),
+            dma((HEADS, 2)), dma((HEADS, 2)), dma((HEADS,)), dma((HEADS,)),
+            dma((HEADS, 2, TP - 1)), dma((HEADS, 2, TP - 1)), dma((HEADS, 6)),
         ],
         compiler_params=pltpu.CompilerParams(
             collective_id=0, has_side_effects=True, vmem_limit_bytes=63 * 2**20),

time: 101 us -> 99.7 us (0.987)
  no operation moved by 1% of the time
where the time goes in v4:
time: 99.7 us; the launch traced here: 99.6 us
  Pallas kernels  97 us (97%)
  other arithmetic  1.87 us (2%)
    pallas_call x1, Pallas kernels, per_device(): pl.pallas_call(kernel, out_shape=jax.ShapeDtypeStruct((2 * ROWS, COLS), F...  97 us

profile of v4, /device:TPU:1, one launch (start us, length us, event | category | flops | bytes accessed | tf_op | source)
XLA Modules:
  0.0 99.6 jit_solution(8054179204104956821)
XLA Ops:
  0.6 0.0 copy-start
  0.6 0.0 copy-start.2
  0.7 0.0 copy-start.1
  0.7 97.0 %attention.1 = f32[256,640]{1,0:T(8,128)} custom-call(bf16[128,384]{1,0:T(8,128)(2,1)} %q_ref.1, bf16[128,384]{1,0:T(8,128)(2,1)} %qt_ref.1, bf16[128,384]{1,0:T(8,128)(2,1)} %k_ref.1, bf16[128,384]{1,0:T(8,128)(2,1)} %kt_ref.1, bf16[128,384]{1,0:T(8,128)(2,1)} %v_ref.1, bf16[128,384]{1,0:T(8,128)(2,1)} %vt_ref.1, bf16[3,128,5120]{2,1,0:T(8,128)(2,1)} %bitcast.1), custom_call_target="tpu_custom_call" | custom-call | tf_op jit(solution)/shard_map/attention/pallas_call | solution.py:352
  97.7 0.0 copy-done
  97.7 0.0 copy-done.2
  97.7 0.0 copy-done.1
  97.7 1.9 %add_convert_fusion = (bf16[128,640]{1,0:T(8,128)(2,1)}, bf16[128,640]{1,0:T(8,128)(2,1)}) fusion(f32[256,640]{1,0:T(8,128)} %attention.1, f32[640]{0:T(1024)S(1)} %copy-done, f32[640]{0:T(1024)S(1)} %copy-done.1, f32[640]{0:T(1024)S(1)} %copy-done.2), kind=kLoop, calls=%fused_computation | loop fusion | flops 573440 | bytes 990720 | tf_op jit(solution)/shard_map/convert_element_type | solution.py:386
Async XLA Ops:
  0.6 97.0 %copy-start = (f32[640]{0:T(1024)S(1)}, f32[640]{0:T(1024)}, u32[]{:S(2)}) copy-start(f32[640]{0:T(1024)} %param.19) | copy-start | bytes 7684
  0.6 97.0 %copy-start.2 = (f32[640]{0:T(1024)S(1)}, f32[640]{0:T(1024)}, u32[]{:S(2)}) copy-start(f32[640]{0:T(1024)} %param.18) | copy-start | bytes 7684
  0.7 97.0 %copy-start.1 = (f32[640]{0:T(1024)S(1)}, f32[640]{0:T(1024)}, u32[]{:S(2)}) copy-start(f32[640]{0:T(1024)} %param.17) | copy-start | bytes 7684

commit v5 on v4

--- a/solution.py
+++ b/solution.py
@@ -141,9 +141,6 @@
             start_ring(h)
     for h in range(HEADS):
         q_copy(h).start()
-    for i in range(TP - 1):
-        w_copy(i).start()
-    own_w.start()
 
     def attend(h, block, first=False):
         pair = qbuf[h]
@@ -304,8 +301,11 @@
         for h in range(HEADS - 1):
             pl.when(k == STEPS + OFFSET[h] + 1)(lambda h=h: join(h))
 
-    for k in range(1, 3):
-        slot(k, False)
+    slot(1, False)
+    for i in range(TP - 1):
+        w_copy(i).start()
+    own_w.start()
+    slot(2, False)
     for i in range(HEADS):
         q_copy(i).wait_recv()
     for h in range(HEADS):

time: 99.7 us -> 99.7 us (level)
  no operation moved by 1% of the time
where the time goes in v5:
time: 99.7 us; the launch traced here: 99.6 us
  Pallas kernels  97 us (97%)
  other arithmetic  1.87 us (2%)
    pallas_call x1, Pallas kernels, per_device(): pl.pallas_call(kernel, out_shape=jax.ShapeDtypeStruct((2 * ROWS, COLS), F...  97 us

profile of v5, /device:TPU:1, one launch (start us, length us, event | category | flops | bytes accessed | tf_op | source)
XLA Modules:
  0.0 99.6 jit_solution(8327851562538212134)
XLA Ops:
  0.6 0.0 copy-start
  0.6 0.0 copy-start.2
  0.7 0.0 copy-start.1
  0.7 97.0 %attention.1 = f32[256,640]{1,0:T(8,128)} custom-call(bf16[128,384]{1,0:T(8,128)(2,1)} %q_ref.1, bf16[128,384]{1,0:T(8,128)(2,1)} %qt_ref.1, bf16[128,384]{1,0:T(8,128)(2,1)} %k_ref.1, bf16[128,384]{1,0:T(8,128)(2,1)} %kt_ref.1, bf16[128,384]{1,0:T(8,128)(2,1)} %v_ref.1, bf16[128,384]{1,0:T(8,128)(2,1)} %vt_ref.1, bf16[3,128,5120]{2,1,0:T(8,128)(2,1)} %bitcast.1), custom_call_target="tpu_custom_call" | custom-call | tf_op jit(solution)/shard_map/attention/pallas_call | solution.py:352
  97.7 0.0 copy-done
  97.7 0.0 copy-done.2
  97.7 0.0 copy-done.1
  97.7 1.9 %add_convert_fusion = (bf16[128,640]{1,0:T(8,128)(2,1)}, bf16[128,640]{1,0:T(8,128)(2,1)}) fusion(f32[256,640]{1,0:T(8,128)} %attention.1, f32[640]{0:T(1024)S(1)} %copy-done, f32[640]{0:T(1024)S(1)} %copy-done.1, f32[640]{0:T(1024)S(1)} %copy-done.2), kind=kLoop, calls=%fused_computation | loop fusion | flops 573440 | bytes 990720 | tf_op jit(solution)/shard_map/convert_element_type | solution.py:386
Async XLA Ops:
  0.6 97.0 %copy-start = (f32[640]{0:T(1024)S(1)}, f32[640]{0:T(1024)}, u32[]{:S(2)}) copy-start(f32[640]{0:T(1024)} %param.19) | copy-start | bytes 7684
  0.6 97.0 %copy-start.2 = (f32[640]{0:T(1024)S(1)}, f32[640]{0:T(1024)}, u32[]{:S(2)}) copy-start(f32[640]{0:T(1024)} %param.18) | copy-start | bytes 7684
  0.7 97.0 %copy-start.1 = (f32[640]{0:T(1024)S(1)}, f32[640]{0:T(1024)}, u32[]{:S(2)}) copy-start(f32[640]{0:T(1024)} %param.17) | copy-start | bytes 7684
